TPU v7x, 32 devices: a whole 2x2x4 slice. The times are simulated.
32 devices in a mesh: plane: 16 (over z, y, core), thick: 2 (over x).
Axes of the slice: x: 2, y: 2, z: 4, core: 2. Of those that a mesh axis runs over, the one named last changes fastest.
Arguments:
- solid: int32 [4, 16, 8, 128], P('thick', 'plane'), may hold values 0 or 1
- labels: int32 [4, 16, 8, 128], P('thick', 'plane'), may hold values 0 or 1
- density: float32 [4, 16, 8, 128], P('thick', 'plane'), may hold values from 0.5 to 2
- wettability: float32 [4, 16, 8, 128], P('thick', 'plane'), may hold values from -1 to 1
- direction: float32 [4, 16, 8, 128], P('thick', 'plane'), may hold values from -6 to 6
- pixel_map: int32 [16, 8, 128], P('plane'), may hold values from 0 to 127
Outputs:
- curvature: float32 [4, 16, 8, 128], P('thick', 'plane')
- readings: float32 [16, 8, 128], P('plane')
All inputs are finite; a program needn't handle non-finite values. No bound on the sum of `solid` or of `labels` on one device may be relied on, other than what follows from the above.
Results may differ from a plain program's by a relative error of at most 0.0001.
Values sent between devices are 32-bit elements; how exact they have to be, the bound alone decides.
No kernel may reach another device: no remote copies, remote signals or barrier semaphores. Data moves between devices by JAX's collectives and lax.ppermute only.
A program may use at most 64 MiB of HBM per device.

v0:
```python
import functools

import jax
import jax.numpy as jnp
import numpy as np
from jax import lax
from jax.experimental import pallas as pl
from jax.experimental.pallas import tpu as pltpu
from jax.sharding import PartitionSpec as P

NBX = 8
STEPS = 2


VELOCITIES = np.array(
    [
        [0, 0, 0],
        [1, 0, 0],
        [-1, 0, 0],
        [0, 1, 0],
        [0, -1, 0],
        [0, 0, 1],
        [0, 0, -1],
        [1, 1, 0],
        [-1, -1, 0],
        [1, -1, 0],
        [-1, 1, 0],
        [1, 0, 1],
        [-1, 0, -1],
        [1, 0, -1],
        [-1, 0, 1],
        [0, 1, 1],
        [0, -1, -1],
        [0, 1, -1],
        [0, -1, 1],
    ]
)
WEIGHTS = np.array([1.0 / 3.0] + [1.0 / 18.0] * 6 + [1.0 / 36.0] * 12)
OPPOSITE = [int(np.argmin(np.abs(VELOCITIES + lattice_vec).sum(1))) for lattice_vec in VELOCITIES]
RELAX_RATE = 1.25
SURFACE_TENSION = 0.2
RECOLOURING_PACE = 0.7


def shifted(array, axis, by):
    devices = lax.axis_size(axis)
    pairs = [(i, i + by) for i in range(devices) if 0 <= i + by < devices]
    return lax.ppermute(array, axis, pairs)


def from_behind(block, axis, distance):
    devices = range(lax.axis_size(axis))
    route = [((i - distance) % len(devices), i) for i in devices]
    return lax.ppermute(block, axis, route)


def weights_like(array):
    return jnp.asarray(WEIGHTS, jnp.float32).reshape((19,) + (1,) * (array.ndim - 1))


def collide(red_pop, blue_pop, gradient, solid_cell):
    lattice_vel = jnp.asarray(VELOCITIES, jnp.float32)
    weight_column_vec = weights_like(red_pop)
    red_density_total = jnp.sum(red_pop, 0)
    blue_density_total = jnp.sum(blue_pop, 0)
    density = red_density_total + blue_density_total
    reciprocal_value = 1.0 / (density + solid_cell)
    total_pop = red_pop + blue_pop
    velocity = (
        jnp.einsum("qd,q...->d...", lattice_vel, total_pop, precision=lax.Precision.HIGHEST)
        * reciprocal_value
    )
    projected = jnp.einsum("qd,d...->q...", lattice_vel, velocity, precision=lax.Precision.HIGHEST)
    speed_sq = jnp.sum(velocity * velocity, 0)
    equilibrium = (
        weight_column_vec
        * density
        * (1.0 + 3.0 * projected + 4.5 * projected * projected - 1.5 * speed_sq)
    )
    relaxed_populations = total_pop + RELAX_RATE * (equilibrium - total_pop)
    along_gradient_dir = jnp.einsum(
        "qd,d...->q...", lattice_vel, gradient, precision=lax.Precision.HIGHEST
    )
    grad_sq = jnp.sum(gradient * gradient, 0)
    norm_scale_factor = 1.0 / jnp.sqrt(1.0 + grad_sq)
    relaxed_populations = (
        relaxed_populations
        + SURFACE_TENSION
        * weight_column_vec
        * (along_gradient_dir * along_gradient_dir - grad_sq / 3.0)
        * norm_scale_factor
    )
    red_output_pop = (
        red_density_total * reciprocal_value * relaxed_populations
        + RECOLOURING_PACE
        * red_density_total
        * blue_density_total
        * reciprocal_value
        * weight_column_vec
        * along_gradient_dir
        * norm_scale_factor
    )
    return (red_output_pop, relaxed_populations - red_output_pop)


def phase_of(red_pop, blue_pop, solid_cell):
    red_density_total = jnp.sum(red_pop, 0)
    blue_density_total = jnp.sum(blue_pop, 0)
    return (red_density_total - blue_density_total) / (
        red_density_total + blue_density_total + solid_cell
    )


def pull_from(padded, offset, extent):
    shift_z, shift_x, shift_y = (int(offset[0]), int(offset[1]), int(offset[2]))
    return padded[
        ...,
        1 - shift_z : 1 - shift_z + extent[0],
        1 - shift_x : 1 - shift_x + extent[1],
        1 - shift_y : 1 - shift_y + extent[2],
    ]


def gradient_of(padded, extent):
    components = [0.0, 0.0, 0.0]
    for number in range(1, 19):
        lattice_vec = VELOCITIES[number]
        pulled = pull_from(padded, -lattice_vec, extent)
        for axis_num in range(3):
            if lattice_vec[axis_num] != 0:
                components[axis_num] = (
                    components[axis_num]
                    + 3.0 * WEIGHTS[number] * float(lattice_vec[axis_num]) * pulled
                )
    return jnp.stack(components)


def spread_back(padded_bar, extent):
    total_bar = 0.0
    for number in range(1, 19):
        lattice_vec = VELOCITIES[number]
        for axis_num in range(3):
            if lattice_vec[axis_num] != 0:
                total_bar = total_bar + 3.0 * WEIGHTS[number] * float(
                    lattice_vec[axis_num]
                ) * pull_from(padded_bar[axis_num], lattice_vec, extent)
    return total_bar


def stream(padded_pop, local_pop, padded_fluid, fluid_cell, extent):
    outgoing = []
    for number in range(19):
        lattice_vec = VELOCITIES[number]
        source_fluid = pull_from(padded_fluid, lattice_vec, extent)
        arrived = pull_from(padded_pop[number], lattice_vec, extent)
        outgoing.append(
            fluid_cell
            * (source_fluid * arrived + (1.0 - source_fluid) * local_pop[OPPOSITE[number]])
        )
    return jnp.stack(outgoing)


def unstream(padded_bar, local_bar, padded_fluid, fluid_cell, extent):
    incoming = []
    for number in range(19):
        lattice_vec = VELOCITIES[number]
        ahead_fluid = pull_from(padded_fluid, -lattice_vec, extent)
        ahead_bar = pull_from(padded_bar[number], -lattice_vec, extent)
        incoming.append(fluid_cell * ahead_bar + (1.0 - ahead_fluid) * local_bar[OPPOSITE[number]])
    return jnp.stack(incoming)


def fill_border(received, chosen, channels):
    if len(chosen) == channels:
        return received
    return (
        jnp.zeros((channels,) + received.shape[1:], received.dtype)
        .at[np.array(chosen)]
        .set(received)
    )


def grow(stacked, axis_dim, chosen_low, chosen_high, sender):
    length = stacked.shape[axis_dim]
    channels = stacked.shape[0]
    borders = []
    for toward in (1, -1):
        chosen = chosen_low if toward == 1 else chosen_high
        source = length - 1 if toward == 1 else 0
        outer_layer = lax.slice_in_dim(stacked, source, source + 1, axis=axis_dim)
        if len(chosen) < channels:
            outer_layer = outer_layer[np.array(chosen)]
        borders.append(fill_border(sender(outer_layer, toward), chosen, channels))
    return jnp.concatenate([borders[0], stacked, borders[1]], axis_dim)


def per_device(solid, labels, density, wettability, direction, pixel_map):
    solid_cell = solid[:, 0].astype(jnp.float32)
    fluid_cell = 1.0 - solid_cell
    label_cell = labels[:, 0].astype(jnp.float32)
    density_cell = density[:, 0]
    wetting = wettability[:, 0]
    tangent = direction[:, 0]
    column_map = pixel_map[0]
    extent = solid_cell.shape
    bricks_y = lax.axis_size("plane") // NBX

    def extend(stacked):
        channels = stacked.shape[0]

        def chosen_for():
            return list(range(channels))

        stacked = grow(
            stacked,
            1,
            chosen_for(),
            chosen_for(),
            lambda outgoing, toward: shifted(outgoing, "thick", toward),
        )
        stacked = grow(
            stacked,
            2,
            chosen_for(),
            chosen_for(),
            lambda outgoing, toward: from_behind(outgoing, "plane", toward * bricks_y),
        )
        stacked = grow(
            stacked,
            3,
            chosen_for(),
            chosen_for(),
            lambda outgoing, toward: from_behind(outgoing, "plane", toward),
        )
        return stacked

    def phase_pair(red_in, blue_in):
        return phase_of(red_in, blue_in, solid_cell)

    def collide_local(red_in, blue_in, gradient):
        return collide(red_in, blue_in, gradient, solid_cell)

    padded_fluid = extend(fluid_cell[None])[0]
    weight_column_vec = weights_like(solid_cell[None])
    red_pop = weight_column_vec * (density_cell * label_cell * fluid_cell)[None]
    blue_pop = weight_column_vec * (density_cell * (1.0 - label_cell) * fluid_cell)[None]
    red_tan = jnp.zeros_like(red_pop)
    blue_tan = jnp.zeros_like(blue_pop)
    checkpoints = []
    for number in range(STEPS):
        phase_val, phase_tan = jax.jvp(phase_pair, (red_pop, blue_pop), (red_tan, blue_tan))
        phase_field = fluid_cell * phase_val + solid_cell * wetting
        field_tan = fluid_cell * phase_tan + solid_cell * tangent
        padded = extend(jnp.stack([phase_field, field_tan]))
        gradient = gradient_of(padded[0], extent)
        gradient_tan = gradient_of(padded[1], extent)
        checkpoints.append((red_pop, blue_pop, gradient))
        (red_post, blue_post), (red_dot, blue_dot) = jax.jvp(
            collide_local, (red_pop, blue_pop, gradient), (red_tan, blue_tan, gradient_tan)
        )
        posted = jnp.concatenate([red_post, blue_post, red_dot, blue_dot])
        moved = extend(posted)
        red_pop, blue_pop, red_tan, blue_tan = [
            stream(
                moved[19 * group : 19 * group + 19],
                posted[19 * group : 19 * group + 19],
                padded_fluid,
                fluid_cell,
                extent,
            )
            for group in range(4)
        ]
    _, phase_tan = jax.jvp(phase_pair, (red_pop, blue_pop), (red_tan, blue_tan))
    partial_sum = jnp.sum(fluid_cell * phase_tan, 0)
    column_sum = lax.psum(partial_sum, "thick")
    found = jnp.take_along_axis(column_sum, column_map, axis=1)
    row_ids = jnp.arange(column_map.shape[0])[:, None]
    seeded = jnp.zeros_like(column_sum).at[row_ids, column_map].add(found)
    _, phase_back = jax.vjp(phase_pair, red_pop, blue_pop)
    red_bar, blue_bar = phase_back(fluid_cell * seeded[None])
    wetting_bar = jnp.zeros_like(wetting)
    for number in reversed(range(STEPS)):
        red_saved, blue_saved, gradient = checkpoints[number]
        outgoing_bar = jnp.concatenate([red_bar, blue_bar]) * fluid_cell
        padded = extend(outgoing_bar)
        red_pre = unstream(padded[:19], outgoing_bar[:19], padded_fluid, fluid_cell, extent)
        blue_pre = unstream(padded[19:], outgoing_bar[19:], padded_fluid, fluid_cell, extent)
        _, collide_back = jax.vjp(collide_local, red_saved, blue_saved, gradient)
        red_bar, blue_bar, gradient_bar = collide_back((red_pre, blue_pre))
        padded_bar = extend(gradient_bar)
        field_bar = spread_back(padded_bar, extent)
        wetting_bar = wetting_bar + solid_cell * field_bar
        if number > 0:
            _, phase_back = jax.vjp(phase_pair, red_saved, blue_saved)
            extra_red, extra_blue = phase_back(fluid_cell * field_bar)
            red_bar = red_bar + extra_red
            blue_bar = blue_bar + extra_blue
    return (wetting_bar[:, None], found[None])


HALF = 128
GROUP = 32
EDGE = 8
ROW_TILES = 3
CZ = [int(v[0]) for v in VELOCITIES]
CX = [int(v[1]) for v in VELOCITIES]
CY = [int(v[2]) for v in VELOCITIES]
GROUPS = [(gx, gy) for gx in (-1, 0, 1) for gy in (-1, 0, 1)]


def lanes():
    return lax.broadcasted_iota(jnp.int32, (8, HALF), 1)


def rows():
    return lax.broadcasted_iota(jnp.int32, (8, HALF), 0)


def turn(tile, by):
    by = by % HALF
    return pltpu.roll(tile, by, 1) if by else tile


def each(function, *fields):
    return [[function(*tiles) for tiles in zip(*units)] for units in zip(*fields)]


def add(a, b):
    return a + b


def sub(a, b):
    return a - b


def read(ref):
    return [[ref[r, u] for u in range(ref.shape[1])] for r in range(ref.shape[0])]


def narrow(field):
    near = rows() < 4
    return [field[0], [jnp.where(near, a, b) for a, b in zip(field[1], field[2])]]


def read_narrow(ref):
    return narrow(read(ref))


def z_shift(field, dz, fill=True):
    out = []
    for units in field:
        layers, side = units[:-1], units[-1]
        zero = jnp.zeros((8, HALF), jnp.float32)
        moved = layers[1:] + [zero] if dz == 1 else [zero] + layers[:-1]
        side = turn(side, -GROUP * dz)
        if fill:
            inside = lanes() < HALF - GROUP if dz == 1 else lanes() >= GROUP
            side = jnp.where(inside, side, 0.0)
        out.append(moved + [side])
    return out


def x_shift(field, dx):
    count = len(field)
    at_edge = rows() == (0 if dx == 1 else 7)
    return [
        [
            pltpu.roll(jnp.where(at_edge, beyond, here), (-dx) % 8, 0)
            for here, beyond in zip(field[r], field[(r + dx) % count])
        ]
        for r in range(count)
    ]


def y_shift(field, dy):
    lane = lanes()
    out = []
    for units in field:
        layers, side = units[:-1], units[-1]
        moved = []
        if dy == 1:
            inner = turn(side, -1)
            for z, tile in enumerate(layers):
                beyond = turn(side, HALF - 1 - (GROUP * z + GROUP - EDGE))
                moved.append(jnp.where(lane == HALF - 1, beyond, turn(tile, -1)))
                at = GROUP * z + EDGE - 1
                inner = jnp.where(lane == at, turn(tile, at), inner)
        else:
            inner = turn(side, 1)
            for z, tile in enumerate(layers):
                beyond = turn(side, -(GROUP * z + EDGE - 1))
                moved.append(jnp.where(lane == 0, beyond, turn(tile, 1)))
                at = GROUP * z + GROUP - EDGE
                inner = jnp.where(lane == at, turn(tile, at + 1), inner)
        out.append(moved + [inner])
    return out


def y_both(field):
    lane = lanes()
    spot = lane & (GROUP - 1)
    ahead, behind = [], []
    for units in field:
        layers, side = units[:-1], units[-1]
        edges = None
        up, down = [], []
        for z, tile in enumerate(layers):
            at = GROUP * z + EDGE - 1
            turned = turn(tile, at)
            edges = turned if edges is None else jnp.where(lane >= GROUP * z, turned, edges)
            beyond = turn(side, HALF - 1 - (GROUP * z + GROUP - EDGE))
            up.append(jnp.where(lane == HALF - 1, beyond, turn(tile, -1)))
            beyond = turn(side, -(GROUP * z + EDGE - 1))
            down.append(jnp.where(lane == 0, beyond, turn(tile, 1)))
        up.append(jnp.where(spot == EDGE - 1, edges, turn(side, -1)))
        lifted = turn(edges, GROUP - EDGE - (EDGE - 2))
        down.append(jnp.where(spot == GROUP - EDGE, lifted, turn(side, 1)))
        ahead.append(up)
        behind.append(down)
    return ahead, behind


def x_both(field):
    return x_shift(field, 1), x_shift(field, -1)


def z_both(field):
    return z_shift(field, 1), z_shift(field, -1)


def gradient(field):
    ahead, behind = z_both(field)
    two = each(lambda m, u, d: 2.0 * m + (u + d), field, ahead, behind)
    y_sum = each(add, *y_both(field))
    x_sum = each(add, *x_both(field))
    along_x = each(sub, *x_both(each(add, two, y_sum)))
    along_y = each(sub, *y_both(each(add, two, x_sum)))
    flat = each(lambda m, a, b: 2.0 * m + (a + b), field, x_sum, y_sum)
    along_z = each(sub, *z_both(flat))
    return along_z, along_x, along_y


def gradient_back(gz, gx, gy):
    def around(field, first, second):
        s = each(add, *first(field))
        t = each(add, *second(field))
        return each(lambda m, a, b: 2.0 * m + (a + b), field, s, t)

    result = each(sub, *x_both(around(gx, z_both, y_both)))
    result = each(add, result, each(sub, *y_both(around(gy, z_both, x_both))))
    return each(add, result, each(sub, *z_both(around(gz, x_both, y_both))))


def all_moved(field):
    ym = {0: field}
    ym[1], ym[-1] = y_both(field)
    xy = {(0, dy): ym[dy] for dy in ym}
    for dy in ym:
        xy[(1, dy)], xy[(-1, dy)] = x_both(ym[dy])
    out = []
    for i in range(19):
        moved = xy[(CX[i], CY[i])]
        out.append(z_shift(moved, CZ[i], fill=False) if CZ[i] else moved)
    return out


def moved_by(field, dz, dx, dy):
    if dy:
        field = y_shift(field, dy)
    if dx:
        field = x_shift(field, dx)
    if dz:
        field = z_shift(field, dz, fill=False)
    return field


def even_part(base, quad):
    zz, xx, yy, zx, zy, xy = quad
    out = [2.0 * (base + zz), 2.0 * (base + xx), 2.0 * (base + yy)]
    for diagonal, cross in ((zz + xx, zx), (zz + yy, zy), (xx + yy, xy)):
        flat = base + diagonal
        out += [flat + cross, flat - cross]
    return out


def odd_part(vector):
    z, x, y = vector
    return [2.0 * z, 2.0 * x, 2.0 * y, z + x, z - x, z + y, z - y, x + y, x - y]


def squares(vector):
    z, x, y = vector
    return [z * z, x * x, y * y, 2.0 * (z * x), 2.0 * (z * y), 2.0 * (x * y)]


def squares_dot(a, b):
    az, ax, ay = a
    bz, bx, by = b
    return [
        2.0 * (az * bz),
        2.0 * (ax * bx),
        2.0 * (ay * by),
        2.0 * (az * bx + ax * bz),
        2.0 * (az * by + ay * bz),
        2.0 * (ax * by + ay * bx),
    ]


def dot(a, b):
    return a[0] * b[0] + a[1] * b[1] + a[2] * b[2]


def first_moment(values):
    d = [values[2 * p + 1] - values[2 * p + 2] for p in range(9)]
    return (
        d[0] + (d[3] + d[4]) + (d[5] + d[6]),
        d[1] + (d[3] - d[4]) + (d[7] + d[8]),
        d[2] + (d[5] - d[6]) + (d[7] - d[8]),
    )


def weighted_first(values):
    d = [values[2 * p + 1] - values[2 * p + 2] for p in range(9)]
    return (
        2.0 * d[0] + (d[3] + d[4]) + (d[5] + d[6]),
        2.0 * d[1] + (d[3] - d[4]) + (d[7] + d[8]),
        2.0 * d[2] + (d[5] - d[6]) + (d[7] - d[8]),
    )


def weighted_even(rest, pairs):
    axis = [2.0 * pairs[0], 2.0 * pairs[1], 2.0 * pairs[2]]
    zx, zy, xy = pairs[3] + pairs[4], pairs[5] + pairs[6], pairs[7] + pairs[8]
    second = [
        axis[0] + zx + zy,
        axis[1] + zx + xy,
        axis[2] + zy + xy,
        pairs[3] - pairs[4],
        pairs[5] - pairs[6],
        pairs[7] - pairs[8],
    ]
    zeroth = 12.0 * rest + axis[0] + axis[1] + axis[2] + zx + zy + xy
    return zeroth, second


def pair_sums(values):
    return [values[2 * p + 1] + values[2 * p + 2] for p in range(9)]


def times(matrix, vector):
    zz, xx, yy, zx, zy, xy = matrix
    z, x, y = vector
    return (zz * z + zx * x + zy * y, zx * z + xx * x + xy * y, zy * z + xy * x + yy * y)


def total(values):
    values = list(values)
    while len(values) > 1:
        values = [
            values[k] + values[k + 1] if k + 1 < len(values) else values[k]
            for k in range(0, len(values), 2)
        ]
    return values[0]


def norm_parts(g):
    g2 = dot(g, g)
    return g2, lax.rsqrt(1.0 + g2)


def fluid_of(dens):
    return jnp.where(dens == 0.0, 0.0, 1.0)


def scatter_groups(acc, r, u, values, stay):
    side = acc.shape[2] - 1
    for k, (gx, gy) in enumerate(GROUPS):
        level = {CZ[i]: values[i] for i in range(1, 19) if (CX[i], CY[i]) == (gx, gy)}
        if (gx, gy) == (0, 0):
            level[0] = values[0] + stay
        if 1 not in level:
            acc[k, r, u] = level[0]
        elif u == side:
            lane = lanes()
            up = jnp.where(lane >= GROUP, turn(level[1], GROUP), 0.0)
            down = jnp.where(lane < HALF - GROUP, turn(level[-1], -GROUP), 0.0)
            acc[k, r, u] = level[0] + (up + down)
        else:
            acc[k, r, u] = acc[k, r, u] + level[0] if u else level[0]
            if u + 1 < side:
                acc[k, r, u + 1] = level[1]
            if u:
                acc[k, r, u - 1] = acc[k, r, u - 1] + level[-1]


def gathered_sum(acc, first, after_x=lambda field: field):
    by_y = []
    for gy in (-1, 0, 1):
        parts = [read(acc.at[first + GROUPS.index((0, gy))])]
        for gx in (-1, 1):
            parts.append(x_shift(read(acc.at[first + GROUPS.index((gx, gy))]), -gx))
        by_y.append(after_x(each(lambda a, b, c: a + (b + c), *parts)))
    return each(
        lambda a, b, c: b + (a + c), y_shift(by_y[0], 1), by_y[1], y_shift(by_y[2], -1)
    )


def toward_gradient(g, fluid, zeroth, second, first, beta):
    _, n = norm_parts(g)
    trace = zeroth * (1.0 / 3.0)
    shifted = [second[0] - trace, second[1] - trace, second[2] - trace] + list(second[3:])
    yg = times(shifted, g)
    gf = dot(g, first)
    nbar = (SURFACE_TENSION * fluid) * dot(g, yg) + beta * gf
    two_q = (2.0 * SURFACE_TENSION * fluid) * n
    bn = beta * n
    fall = nbar * n * n * n
    return [two_q * y + bn * f - fall * v for y, f, v in zip(yg, first, g)], n * gf


def main_kernel(nz, local_z, qp_ref, sl_ref, qm_ref, q_ref, map_ref, out_ref, read_ref,
                rho, p1, dp1, blk, t_st, dt_st, acc, pop, dpop, mac, p2, dp2, g1, g2, dg,
                a3, b3, adj, gbar, pbar2):
    thick = lax.axis_index("thick")
    even = lax.rem(lax.axis_index("plane"), 2) == 0
    units = nz + 1
    side = nz
    per = 3 * local_z + 1
    edge0 = 2 * per
    spot = lanes() & (GROUP - 1)
    left_part = spot < GROUP // 2

    def edge(ref, k):
        if k == 3:
            return ref[edge0 + k]
        return ref[edge0 + k] + ref[edge0 + 4 + k]

    def beside(r, k):
        own, minus, plus = [functools.partial(edge, ref, k) for ref in (q_ref, qm_ref, qp_ref)]
        corner = functools.partial(edge, sl_ref, k)
        if r == 0:
            right, left = jnp.where(even, own(), plus()), jnp.where(even, minus(), own())
        elif r == 1:
            right, left = jnp.where(even, plus(), corner()), jnp.where(even, own(), plus())
        else:
            right, left = jnp.where(even, minus(), own()), jnp.where(even, corner(), minus())
        return jnp.where(left_part, left, right)

    counts = []
    for r, source in enumerate((q_ref, qp_ref, qm_ref)):
        for which, ref in enumerate((rho, p1, dp1)):
            for z in range(nz):
                slab, zl = divmod(z, local_z)
                start = jnp.where(thick == slab, 0, per)
                ref[r, z] = source[start + which * local_z + zl]
            ref[r, side] = beside(r, which)
        counts.append([source[per - 1], beside(r, 3)])
    counts = narrow(counts)

    fluid_field = each(fluid_of, read(rho))
    ym = {0: fluid_field}
    ym[1], ym[-1] = y_both(fluid_field)
    xy = {(0, dy): ym[dy] for dy in ym}
    for dy in ym:
        xy[(1, dy)], xy[(-1, dy)] = x_both(ym[dy])
    for i in range(1, 19):
        there = xy[(CX[i], CY[i])]
        if CZ[i]:
            there = z_shift(there, CZ[i])
        for r in range(ROW_TILES):
            for u in range(units):
                blk[i - 1, r, u] = 1.0 - fluid_field[r][u] * there[r][u]

    def store_gradient(ref, first, field):
        for k, part in enumerate(gradient(field)):
            for r in range(ROW_TILES):
                for u in range(units):
                    ref[first + k, r, u] = part[r][u] * (1.0 / 12.0)

    store_gradient(g1, 0, read(p1))
    store_gradient(dg, 0, read(dp1))
    for r in range(ROW_TILES):
        for u in range(units):
            dens, psi = rho[r, u], p1[r, u]
            fluid = fluid_of(dens)
            red = 0.5 * dens * (1.0 + psi)
            blue = 0.5 * dens * (1.0 - psi)
            alpha = red / (dens + (1.0 - fluid))
            beta = RECOLOURING_PACE * alpha * blue
            g = [g1[k, r, u] for k in range(3)]
            gd = [dg[k, r, u] for k in range(3)]
            gg, n = norm_parts(g)
            gdg = dot(g, gd)
            n2g = n * n * gdg
            dn = -n * n2g
            q = (SURFACE_TENSION * fluid) * n
            dq = -q * n2g
            sq, dsq = squares(g), squares_dot(g, gd)
            base = dens - q * gg * (1.0 / 3.0)
            dbase = (dq * gg + 2.0 * q * gdg) * (-1.0 / 3.0)
            ev = even_part(base, [q * v for v in sq])
            dev = even_part(dbase, [dq * v + q * d for v, d in zip(sq, dsq)])
            bn, bdn = beta * n, beta * dn
            od = odd_part([bn * v for v in g])
            dod = odd_part([bdn * v + bn * d for v, d in zip(g, gd)])
            for k in range(9):
                t_st[k, r, u] = ev[k]
                dt_st[k, r, u] = dev[k]
            pop[0, r, u] = 12.0 * base
            dpop[0, r, u] = 12.0 * dbase
            s = [None] + [blk[i, r, u] for i in range(18)]
            for first, rest, evens, odds in (
                (0, 12.0 * base, ev, od), (9, 12.0 * dbase, dev, dod)
            ):
                scaled = [alpha * v for v in evens]
                values = [alpha * rest]
                stay = []
                for k in range(9):
                    values += [scaled[k] + odds[k], scaled[k] - odds[k]]
                    stay += [s[2 * k + 1] * values[-2], s[2 * k + 2] * values[-1]]
                scatter_groups(acc.at[pl.ds(first, 9)], r, u, values, total(stay))

    for ref, store in ((t_st, pop), (dt_st, dpop)):
        for k in range(9):
            i = 2 * k + 1
            field = read(ref.at[k])
            ahead, behind = field, field
            if CY[i]:
                ahead, behind = y_both(field)
                if CY[i] == -1:
                    ahead, behind = behind, ahead
            if CX[i]:
                ahead, behind = x_shift(ahead, CX[i]), x_shift(behind, -CX[i])
            if CZ[i]:
                ahead = z_shift(ahead, CZ[i], fill=False)
                behind = z_shift(behind, -CZ[i], fill=False)
            for r in range(ROW_TILES):
                for u in range(units):
                    here = field[r][u]
                    pop_i = jnp.where(blk[i, r, u] > 0.5, here, behind[r][u])
                    pop_o = jnp.where(blk[i - 1, r, u] > 0.5, here, ahead[r][u])
                    store[i, r, u] = pop_i
                    store[i + 1, r, u] = pop_o
    red_sum = gathered_sum(acc, 0)
    dred_sum = gathered_sum(acc, 9)
    for r in range(ROW_TILES):
        for u in range(units):
            fluid = fluid_of(rho[r, u])
            dens = total([pop[i, r, u] for i in range(19)]) * (1.0 / 36.0)
            ddens = total([dpop[i, r, u] for i in range(19)]) * (1.0 / 36.0)
            scale = fluid * (1.0 / 36.0)
            red = red_sum[r][u] * scale
            dred = dred_sum[r][u] * scale
            inv = 1.0 / (dens + (1.0 - fluid))
            psi = (2.0 * red - dens) * inv
            dpsi = (2.0 * dred - (1.0 + psi) * ddens) * inv
            for k, v in enumerate((dens, ddens, red, dred, inv, psi)):
                mac[k, r, u] = v
            p2[r, u] = jnp.where(fluid > 0.5, psi, p1[r, u])
            dp2[r, u] = jnp.where(fluid > 0.5, dpsi, dp1[r, u])

    store_gradient(g2, 0, read(p2))
    store_gradient(dg, 0, read(dp2))
    for r in range(ROW_TILES):
        for u in range(units):
            dens, ddens, red, dred, inv = [mac[k, r, u] for k in range(5)]
            fluid = fluid_of(rho[r, u])
            t = [pop[i, r, u] for i in range(19)]
            dt = [dpop[i, r, u] for i in range(19)]
            m = [v * (1.0 / 36.0) for v in first_moment(t)]
            dm = [v * (1.0 / 36.0) for v in first_moment(dt)]
            vel = [inv * v for v in m]
            shrink = inv * ddens
            dvel = [inv * b - shrink * a for a, b in zip(vel, dm)]
            g = [g2[k, r, u] for k in range(3)]
            gd = [dg[k, r, u] for k in range(3)]
            gg, n = norm_parts(g)
            gdg = dot(g, gd)
            n2g = n * n * gdg
            dn = -n * n2g
            q = (SURFACE_TENSION * fluid) * n
            dq = -q * n2g
            base = RELAX_RATE * dens - (1.5 * RELAX_RATE) * dot(m, vel) - q * gg * (1.0 / 3.0)
            dbase = (
                RELAX_RATE * ddens
                - (1.5 * RELAX_RATE) * (dot(dm, vel) + dot(m, dvel))
                + (dq * gg + 2.0 * q * gdg) * (-1.0 / 3.0)
            )
            lin = odd_part([(3.0 * RELAX_RATE) * v for v in m])
            dlin = odd_part([(3.0 * RELAX_RATE) * v for v in dm])
            mq = [(4.5 * RELAX_RATE) * v for v in m]
            dmq = [(4.5 * RELAX_RATE) * v for v in dm]
            order = ((0, 0), (1, 1), (2, 2), (0, 1), (0, 2), (1, 2))
            sq, dsq = squares(g), squares_dot(g, gd)
            quad, dquad = [], []
            for k, (a, b) in enumerate(order):
                flow = mq[a] * vel[b]
                dflow = dmq[a] * vel[b] + mq[a] * dvel[b]
                if a != b:
                    flow = 2.0 * flow
                    dflow = 2.0 * dflow
                quad.append(flow + q * sq[k])
                dquad.append(dflow + dq * sq[k] + q * dsq[k])
            ev, dev = even_part(base, quad), even_part(dbase, dquad)
            keep = 1.0 - RELAX_RATE
            after, dafter = [keep * t[0] + 12.0 * base], [keep * dt[0] + 12.0 * dbase]
            for k in range(9):
                after += [keep * t[2 * k + 1] + (ev[k] + lin[k]), keep * t[2 * k + 2] + (ev[k] - lin[k])]
                dafter += [
                    keep * dt[2 * k + 1] + (dev[k] + dlin[k]),
                    keep * dt[2 * k + 2] + (dev[k] - dlin[k]),
                ]
            alpha = red * inv
            dalpha = dred * inv - alpha * shrink
            blue, dblue = dens - red, ddens - dred
            beta = RECOLOURING_PACE * alpha * blue
            dbeta = RECOLOURING_PACE * (dalpha * blue + alpha * dblue)
            bn = beta * n
            dbn = dbeta * n + beta * dn
            od = odd_part([bn * v for v in g])
            dod = odd_part([dbn * v + bn * d for v, d in zip(g, gd)])
            reds, dreds = [alpha * after[0]], [dalpha * after[0] + alpha * dafter[0]]
            for i in range(1, 19):
                k = (i - 1) // 2
                side = od[k] if i % 2 else -od[k]
                dside = dod[k] if i % 2 else -dod[k]
                reds.append(alpha * after[i] + side)
                dreds.append(dalpha * after[i] + alpha * dafter[i] + dside)
            s = [None] + [blk[i, r, u] for i in range(18)]
            for k, values in enumerate((reds, dreds, after, dafter)):
                stay = total([s[i] * values[i] for i in range(1, 19)])
                scatter_groups(acc.at[pl.ds(9 * k, 9)], r, u, values, stay)

    red_s = gathered_sum(acc, 0, narrow)
    dred_s = gathered_sum(acc, 9, narrow)
    dens_s = gathered_sum(acc, 18, narrow)
    ddens_s = gathered_sum(acc, 27, narrow)
    rho_n = read_narrow(rho)
    seeds = []
    for r in range(2):
        found, pulls = [], []
        for u in range(units):
            fluid = fluid_of(rho_n[r][u])
            scale = fluid * (1.0 / 36.0)
            dens = dens_s[r][u] * scale
            inv = 1.0 / (dens + (1.0 - fluid))
            psi = (2.0 * (red_s[r][u] * scale) - dens) * inv
            a = 2.0 * (scale * inv)
            b = -(scale * inv) * (1.0 + psi)
            pulls.append((a, b))
            found.append(a * dred_s[r][u] + b * ddens_s[r][u])
        column = total(found[:-1])
        if r == 0:
            read_ref[...] = jnp.take_along_axis(column, map_ref[...], axis=1)
        beside_sum = found[-1] + turn(found[-1], GROUP)
        beside_sum = beside_sum + turn(beside_sum, 2 * GROUP)
        seed = [column * counts[r][0]] * nz + [beside_sum * counts[r][1]]
        for u in range(units):
            a3[r, u] = pulls[u][0] * seed[u]
            b3[r, u] = pulls[u][1] * seed[u]

    def pick(ref, k, r, u):
        if r == 0:
            return ref[k, 0, u]
        return jnp.where(rows() < 4, ref[k, 1, u], ref[k, 2, u])

    ahead_r = all_moved(read(a3))
    ahead_t = all_moved(read(b3))
    for r in range(2):
        for u in range(units):
            own_r, own_t = a3[r, u], b3[r, u]
            dens, red, inv = [pick(mac, k, r, u) for k in (0, 2, 4)]
            fluid = fluid_of(rho_n[r][u])
            alpha = red * inv
            blue = dens - red
            beta = RECOLOURING_PACE * alpha * blue
            r_hat, hat = [own_r], [own_t + alpha * own_r]
            for i in range(1, 19):
                blocked = pick(blk, i - 1, r, u) > 0.5
                r_i = jnp.where(blocked, own_r, ahead_r[i][r][u])
                t_i = jnp.where(blocked, own_t, ahead_t[i][r][u])
                r_hat.append(r_i)
                hat.append(t_i + alpha * r_i)
            t = [pick(pop, i, r, u) for i in range(19)]
            m = [v * (1.0 / 36.0) for v in first_moment(t)]
            vel = [inv * v for v in m]
            g = [pick(g2, k, r, u) for k in range(3)]
            _, n = norm_parts(g)
            q = (SURFACE_TENSION * fluid) * n
            h0, h2 = weighted_even(hat[0], pair_sums(hat))
            h1 = weighted_first(hat)
            k0, k2 = weighted_even(r_hat[0], pair_sums(r_hat))
            k1 = weighted_first(r_hat)
            bars, n_gk = toward_gradient(g, fluid, h0, h2, k1, beta)
            for k in range(3):
                gbar[k, r, u] = bars[k]
            uu = 1.5 * RELAX_RATE
            flow = [(4.5 * RELAX_RATE) * k2[j] - (uu * k0 if j < 3 else 0.0) for j in range(6)]
            surf = [k2[j] - (k0 * (1.0 / 3.0) if j < 3 else 0.0) for j in range(6)]
            alpha_bar = (
                (1.0 - RELAX_RATE) * total([a * b for a, b in zip(r_hat, t)])
                + RELAX_RATE * dens * k0
                + (3.0 * RELAX_RATE) * dot(m, k1)
                + dot(m, times(flow, vel))
                + q * dot(g, times(surf, g))
            )
            alpha_bar = alpha_bar + RECOLOURING_PACE * blue * n_gk
            blue_bar = RECOLOURING_PACE * alpha * n_gk
            flow_h = [(4.5 * RELAX_RATE) * h2[j] - (uu * h0 if j < 3 else 0.0) for j in range(6)]
            xu = times(flow_h, vel)
            red_bar = inv * alpha_bar - blue_bar
            dens_bar = RELAX_RATE * h0 - dot(vel, xu) + blue_bar - alpha * inv * alpha_bar
            adj[19, r, u] = red_bar
            adj[20, r, u] = dens_bar
            for k in range(3):
                adj[21 + k, r, u] = ((3.0 * RELAX_RATE) * h1[k] + 2.0 * xu[k]) * (1.0 / 36.0)
            for i in range(19):
                adj[i, r, u] = hat[i]

    field = gradient_back(*[read(gbar.at[k]) for k in range(3)])
    for r in range(2):
        for u in range(units):
            fluid = fluid_of(rho_n[r][u])
            inv, psi = pick(mac, 4, r, u), pick(mac, 5, r, u)
            bar = field[r][u] * (-1.0 / 12.0)
            if r == 0 and u < nz:
                pbar2[u] = bar
            psi_bar = fluid * bar * inv
            red_bar = adj[19, r, u] + 2.0 * psi_bar
            dens_bar = (adj[20, r, u] - (1.0 + psi) * psi_bar) * (1.0 / 36.0)
            pull = [adj[21 + k, r, u] for k in range(3)]
            push = pull + odd_part(pull)[3:]
            keep = 1.0 - RELAX_RATE
            adj[19, r, u] = red_bar * (1.0 / 36.0)
            adj[0, r, u] = keep * adj[0, r, u] + dens_bar
            for k in range(9):
                adj[2 * k + 1, r, u] = keep * adj[2 * k + 1, r, u] + (dens_bar + push[k])
                adj[2 * k + 2, r, u] = keep * adj[2 * k + 2, r, u] + (dens_bar - push[k])

    ahead_r = all_moved(read(adj.at[19]))
    ahead = [None] + [moved_by(read(adj.at[i]), CZ[i], CX[i], CY[i]) for i in range(1, 19)]
    for r in range(2):
        for u in range(units):
            dens = rho_n[r][u]
            psi = jnp.where(rows() < 4, p1[1, u], p1[2, u]) if r else p1[0, u]
            fluid = fluid_of(dens)
            red = 0.5 * dens * (1.0 + psi)
            blue = 0.5 * dens * (1.0 - psi)
            alpha = red / (dens + (1.0 - fluid))
            beta = RECOLOURING_PACE * alpha * blue
            own = adj[19, r, u]
            r_hat, hat = [own], [adj[0, r, u] + alpha * own]
            for i in range(1, 19):
                blocked = pick(blk, i - 1, r, u) > 0.5
                r_i = jnp.where(blocked, own, ahead_r[i][r][u])
                r_hat.append(r_i)
                hat.append(
                    jnp.where(blocked, adj[OPPOSITE[i], r, u], ahead[i][r][u]) + alpha * r_i
                )
            h0, h2 = weighted_even(hat[0], pair_sums(hat))
            g = [pick(g1, k, r, u) for k in range(3)]
            bars, _ = toward_gradient(g, fluid, h0, h2, weighted_first(r_hat), beta)
            for k in range(3):
                gbar[k, r, u] = bars[k]

    field = gradient_back(*[read(gbar.at[k]) for k in range(3)])
    result = []
    for z in range(nz):
        bar = pbar2[z] + field[0][z] * (-1.0 / 12.0)
        result.append(jnp.where(rho[0, z] == 0.0, bar, 0.0))
    for zl in range(local_z):
        chosen = result[zl]
        for slab in range(1, nz // local_z):
            chosen = jnp.where(thick == slab, result[slab * local_z + zl], chosen)
        out_ref[zl] = chosen


def pack_kernel(nz, local_z, solid_ref, labels_ref, density_ref, wet_ref, dir_ref, map_ref,
                out_ref, edge_ref):
    thick = lax.axis_index("thick")
    lane = lanes()
    spot = lane & (GROUP - 1)
    ends = (spot < EDGE, spot >= GROUP - EDGE)
    zero = jnp.zeros((8, HALF), jnp.float32)
    edges = [zero, zero, zero]

    def place(tile, z, into):
        here = (lane >= GROUP * z) & (lane < GROUP * z + GROUP)
        last = pltpu.roll(tile, lax.rem(GROUP * z + EDGE, HALF), 1)
        first = pltpu.roll(tile, lax.rem(GROUP * z + GROUP - EDGE, HALF), 1)
        into = jnp.where(here & ends[0], last, into)
        return jnp.where(here & ends[1], first, into)

    for zl in range(local_z):
        solid = solid_ref[zl].astype(jnp.float32)
        label = labels_ref[zl].astype(jnp.float32)
        fluid = 1.0 - solid
        red = density_ref[zl] * label * fluid
        blue = density_ref[zl] * (1.0 - label) * fluid
        psi = (red - blue) / (red + blue + solid)
        values = (red + blue, fluid * psi + solid * wet_ref[zl], solid * dir_ref[zl])
        for k, value in enumerate(values):
            out_ref[k * local_z + zl] = value
            edges[k] = place(value, thick * local_z + zl, edges[k])
    pixels = map_ref[...]
    counts = jnp.zeros(pixels.shape, jnp.int32)
    for k in range(pixels.shape[1]):
        counts = counts + (turn(pixels, k) == lane).astype(jnp.int32)
    counts = counts.astype(jnp.float32)
    out_ref[3 * local_z] = counts
    by_layer = zero
    for z in range(nz):
        by_layer = jnp.where(
            (lane >= GROUP * z) & ends[0], turn(counts, GROUP * z + EDGE), by_layer
        )
        by_layer = jnp.where(
            (lane >= GROUP * z) & ends[1], turn(counts, GROUP * z + GROUP - EDGE), by_layer
        )
    for k, tile in enumerate(edges + [by_layer]):
        edge_ref[k] = tile


def one_exchange(solid, labels, density, wettability, direction, pixel_map):
    local_z = solid.shape[0]
    planes, slabs = lax.axis_size("plane"), lax.axis_size("thick")
    nz = local_z * slabs
    per = 3 * local_z + 1
    vmem = pl.BlockSpec(memory_space=pltpu.VMEM)
    packed, edges = pl.pallas_call(
        functools.partial(pack_kernel, nz, local_z),
        out_shape=(
            jax.ShapeDtypeStruct((per, 8, HALF), jnp.float32),
            jax.ShapeDtypeStruct((4, 8, HALF), jnp.float32),
        ),
        in_specs=[vmem] * 6,
        out_specs=(vmem, vmem),
    )(solid[:, 0], labels[:, 0], density[:, 0], wettability[:, 0], direction[:, 0], pixel_map[0])

    def send(array, target):
        route = []
        for b in range(planes):
            for t in range(slabs):
                to_b, to_t = target(b, t)
                route.append((b * slabs + t, (to_b % planes) * slabs + to_t))
        return lax.ppermute(array, ("plane", "thick"), route)

    beside_z = send(packed, lambda b, t: (b, 1 - t))
    beside_y = send(edges, lambda b, t: (b ^ 1, t))
    beside_zy = send(edges, lambda b, t: (b ^ 1, 1 - t))
    quad = jnp.concatenate([packed, beside_z, beside_y, beside_zy])
    above = send(quad, lambda b, t: (b + 2, t))
    below = send(quad, lambda b, t: (b - 2, t))
    corner = send(quad, lambda b, t: (b + 4 if b % 2 == 0 else b - 4, t))

    def field(*lead, tiles=ROW_TILES):
        return pltpu.VMEM(lead + (tiles, nz + 1, 8, HALF), jnp.float32)

    return pl.pallas_call(
        functools.partial(main_kernel, nz, local_z),
        out_shape=(
            jax.ShapeDtypeStruct((local_z, 8, HALF), jnp.float32),
            jax.ShapeDtypeStruct((8, HALF), jnp.float32),
        ),
        in_specs=[vmem] * 5,
        out_specs=(vmem, vmem),
        scratch_shapes=[
            field(), field(), field(), field(18), field(9), field(9), field(36),
            field(19), field(19), field(6), field(), field(), field(3), field(3), field(3),
            field(tiles=2), field(tiles=2), field(24, tiles=2), field(3, tiles=2),
            pltpu.VMEM((nz, 8, HALF), jnp.float32),
        ],
        compiler_params=pltpu.CompilerParams(vmem_limit_bytes=24 * 1024 * 1024),
    )(below, corner, above, quad, pixel_map[0])


def fits_one_exchange(mesh, solid):
    sizes = (mesh.shape["plane"], mesh.shape["thick"])
    return sizes == (2 * NBX, 2) and solid.shape[2:] == (8, HALF) and solid.shape[0] * GROUP == HALF


def solution(mesh):
    specs = (P("thick", "plane", None, None),) * 5 + (P("plane", None, None),)
    out_specs = (P("thick", "plane", None, None), P("plane", None, None))

    def program(solid, *rest):
        def with_bricks(*blocks):
            curvature, readings = one_exchange(*blocks)
            return curvature[:, None], readings[None]

        body = with_bricks if fits_one_exchange(mesh, solid) else per_device
        return jax.shard_map(
            body, mesh=mesh, in_specs=specs, out_specs=out_specs, check_vma=False
        )(solid, *rest)

    return program
```

profile of v0, /device:TPU:0, one launch (start us, length us, event | category | flops | bytes accessed | tf_op | source)
XLA Modules:
  0.0 28.4 jit_solution(7605852608991244948)
XLA Ops:
  0.6 1.7 %shard_map.77 = (f32[7,8,128]{2,1,0:T(8,128)}, f32[4,8,128]{2,1,0:T(8,128)}) custom-call(s32[2,8,128]{2,1,0:T(8,128)} %bitcast.12, s32[2,8,128]{2,1,0:T(8,128)} %bitcast.13, f32[2,8,128]{2,1,0:T(8,128)} %bitcast.14, f32[2,8,128]{2,1,0:T(8,128)} %bitcast.15, f32[2,8,128]{2,1,0:T(8,128)} %bitcast.16, s32[8,128]{1,0:T(8,128)} %bitcast.10), custom_call_target="tpu_custom_call" | custom-call | tf_op jit(solution)/shard_map/pallas_call | solution.py:1029
  2.3 2.4 %collective-permute-start.2 = (f32[4,8,128]{2,1,0:T(8,128)}, f32[4,8,128]{2,1,0:T(8,128)S(1)}, u32[]{:S(2)}, u32[]{:S(2)}) collective-permute-start(f32[4,8,128]{2,1,0:T(8,128)} %get-tuple-element.7), channel_id=1, source_target_pairs={{0,3},{1,2},{2,1},{3,0},{4,7},{5,6},{6,5},{7,4},{8,11},{9,10},{10,... | collective-permute-start | bytes 49160 | tf_op jit(solution)/shard_map/ppermute | solution.py:1045
  4.7 0.7 %collective-permute-start.1 = (f32[4,8,128]{2,1,0:T(8,128)}, f32[4,8,128]{2,1,0:T(8,128)S(1)}, u32[]{:S(2)}, u32[]{:S(2)}) collective-permute-start(f32[4,8,128]{2,1,0:T(8,128)} %get-tuple-element.7), channel_id=1, source_target_pairs={{0,2},{1,3},{2,0},{3,1},{4,6},{5,7},{6,4},{7,5},{8,10},{9,11},{10,... | collective-permute-start | bytes 49160 | tf_op jit(solution)/shard_map/ppermute | solution.py:1045
  5.3 0.0 collective-permute-start
  5.4 0.8 %constant_dynamic-update-slice_fusion.3 = f32[22,8,128]{2,1,0:T(8,128)S(1)} fusion(f32[7,8,128]{2,1,0:T(8,128)} %get-tuple-element.6), kind=kLoop, calls=%fused_computation.3 | loop fusion | bytes 57344
  6.1 3.3 %collective-permute-done = f32[7,8,128]{2,1,0:T(8,128)S(1)} collective-permute-done((f32[7,8,128]{2,1,0:T(8,128)}, f32[7,8,128]{2,1,0:T(8,128)S(1)}, u32[]{:S(2)}, u32[]{:S(2)}) %collective-permute-start) | collective-permute-done | bytes 28704 | tf_op jit(solution)/shard_map/ppermute | solution.py:1045
  9.4 0.0 collective-permute-done.1
  9.4 0.0 copy-start
  9.5 0.0 collective-permute-done.2
  9.5 1.6 %collective-permute-start.5 = (f32[22,8,128]{2,1,0:T(8,128)S(1)}, f32[22,8,128]{2,1,0:T(8,128)S(1)}, u32[]{:S(2)}, u32[]{:S(2)}) collective-permute-start(f32[22,8,128]{2,1,0:T(8,128)S(1)} %constant_dynamic-update-slice_fusion.q_ref), channel_id=1, source_target_pairs={{0,4},{1,5},{2,6},{3,7},{4,8},{5,9},{6,10},{7,11},{8,12},{9,13},{1... | collective-permute-start | bytes 270344 | tf_op jit(solution)/shard_map/ppermute | solution.py:1045
  11.0 1.6 %collective-permute-start.4 = (f32[22,8,128]{2,1,0:T(8,128)S(1)}, f32[22,8,128]{2,1,0:T(8,128)S(1)}, u32[]{:S(2)}, u32[]{:S(2)}) collective-permute-start(f32[22,8,128]{2,1,0:T(8,128)S(1)} %constant_dynamic-update-slice_fusion.q_ref), channel_id=1, source_target_pairs={{0,8},{1,9},{2,26},{3,27},{4,12},{5,13},{6,30},{7,31},{8,16},{9,17... | collective-permute-start | bytes 270344 | tf_op jit(solution)/shard_map/ppermute | solution.py:1045
  12.6 3.2 %collective-permute-start.3 = (f32[22,8,128]{2,1,0:T(8,128)S(1)}, f32[22,8,128]{2,1,0:T(8,128)S(1)}, u32[]{:S(2)}, u32[]{:S(2)}) collective-permute-start(f32[22,8,128]{2,1,0:T(8,128)S(1)} %constant_dynamic-update-slice_fusion.q_ref), channel_id=1, source_target_pairs={{0,28},{1,29},{2,30},{3,31},{4,0},{5,1},{6,2},{7,3},{8,4},{9,5},{1... | collective-permute-start | bytes 270344 | tf_op jit(solution)/shard_map/ppermute | solution.py:1045
  15.8 1.4 %collective-permute-done.5.qm_ref = f32[22,8,128]{2,1,0:T(8,128)S(1)} collective-permute-done((f32[22,8,128]{2,1,0:T(8,128)S(1)}, f32[22,8,128]{2,1,0:T(8,128)S(1)}, u32[]{:S(2)}, u32[]{:S(2)}) %collective-permute-start.5) | collective-permute-done | bytes 90144 | tf_op jit(solution)/shard_map/ppermute | solution.py:1045
  17.2 0.2 collective-permute-done.4.sl_ref
  17.4 1.0 %collective-permute-done.3.qp_ref = f32[22,8,128]{2,1,0:T(8,128)S(1)} collective-permute-done((f32[22,8,128]{2,1,0:T(8,128)S(1)}, f32[22,8,128]{2,1,0:T(8,128)S(1)}, u32[]{:S(2)}, u32[]{:S(2)}) %collective-permute-start.3) | collective-permute-done | bytes 90144 | tf_op jit(solution)/shard_map/ppermute | solution.py:1045
  18.4 0.0 copy-done
  18.4 9.9 %shard_map.78 = (f32[2,8,128]{2,1,0:T(8,128)}, f32[8,128]{1,0:T(8,128)}) custom-call(f32[22,8,128]{2,1,0:T(8,128)S(1)} %collective-permute-done.3.qp_ref, f32[22,8,128]{2,1,0:T(8,128)S(1)} %collective-permute-done.4.sl_ref, f32[22,8,128]{2,1,0:T(8,128)S(1)} %collective-permute-done.5.qm_ref, f32[22,8,128]{2,1,0:T(8,128)S(1)} %constant_dynamic-update-slice_fusion.q_ref, ...), custom_call_target="tpu_custom_call" | custom-call | tf_op jit(solution)/shard_map/pallas_call | solution.py:1058
  (3 shorter events, 0.0 us)
Async XLA Ops:
  2.3 7.2 %collective-permute-start.2 = (f32[4,8,128]{2,1,0:T(8,128)}, f32[4,8,128]{2,1,0:T(8,128)S(1)}, u32[]{:S(2)}, u32[]{:S(2)}) collective-permute-start(f32[4,8,128]{2,1,0:T(8,128)} %get-tuple-element.7), channel_id=1, source_target_pairs={{0,3},{1,2},{2,1},{3,0},{4,7},{5,6},{6,5},{7,4},{8,11},{9,10},{10,... | collective-permute-start | bytes 49160 | tf_op jit(solution)/shard_map/ppermute | solution.py:1045
  4.7 4.8 %collective-permute-start.1 = (f32[4,8,128]{2,1,0:T(8,128)}, f32[4,8,128]{2,1,0:T(8,128)S(1)}, u32[]{:S(2)}, u32[]{:S(2)}) collective-permute-start(f32[4,8,128]{2,1,0:T(8,128)} %get-tuple-element.7), channel_id=1, source_target_pairs={{0,2},{1,3},{2,0},{3,1},{4,6},{5,7},{6,4},{7,5},{8,10},{9,11},{10,... | collective-permute-start | bytes 49160 | tf_op jit(solution)/shard_map/ppermute | solution.py:1045
  5.3 4.1 %collective-permute-start = (f32[7,8,128]{2,1,0:T(8,128)}, f32[7,8,128]{2,1,0:T(8,128)S(1)}, u32[]{:S(2)}, u32[]{:S(2)}) collective-permute-start(f32[7,8,128]{2,1,0:T(8,128)} %get-tuple-element.6), channel_id=1, source_target_pairs={{0,1},{1,0},{2,3},{3,2},{4,5},{5,4},{6,7},{7,6},{8,9},{9,8},{10,11... | collective-permute-start | bytes 86024 | tf_op jit(solution)/shard_map/ppermute | solution.py:1045
  9.4 9.0 %copy-start = (s32[1,8,128]{2,1,0:T(8,128)S(1)}, s32[1,8,128]{2,1,0:T(8,128)}, u32[]{:S(2)}) copy-start(s32[1,8,128]{2,1,0:T(8,128)} %param.11) | copy-start | bytes 12292
  9.5 7.7 %collective-permute-start.5 = (f32[22,8,128]{2,1,0:T(8,128)S(1)}, f32[22,8,128]{2,1,0:T(8,128)S(1)}, u32[]{:S(2)}, u32[]{:S(2)}) collective-permute-start(f32[22,8,128]{2,1,0:T(8,128)S(1)} %constant_dynamic-update-slice_fusion.q_ref), channel_id=1, source_target_pairs={{0,4},{1,5},{2,6},{3,7},{4,8},{5,9},{6,10},{7,11},{8,12},{9,13},{1... | collective-permute-start | bytes 270344 | tf_op jit(solution)/shard_map/ppermute | solution.py:1045
  11.0 6.3 %collective-permute-start.4 = (f32[22,8,128]{2,1,0:T(8,128)S(1)}, f32[22,8,128]{2,1,0:T(8,128)S(1)}, u32[]{:S(2)}, u32[]{:S(2)}) collective-permute-start(f32[22,8,128]{2,1,0:T(8,128)S(1)} %constant_dynamic-update-slice_fusion.q_ref), channel_id=1, source_target_pairs={{0,8},{1,9},{2,26},{3,27},{4,12},{5,13},{6,30},{7,31},{8,16},{9,17... | collective-permute-start | bytes 270344 | tf_op jit(solution)/shard_map/ppermute | solution.py:1045
  12.6 5.8 %collective-permute-start.3 = (f32[22,8,128]{2,1,0:T(8,128)S(1)}, f32[22,8,128]{2,1,0:T(8,128)S(1)}, u32[]{:S(2)}, u32[]{:S(2)}) collective-permute-start(f32[22,8,128]{2,1,0:T(8,128)S(1)} %constant_dynamic-update-slice_fusion.q_ref), channel_id=1, source_target_pairs={{0,28},{1,29},{2,30},{3,31},{4,0},{5,1},{6,2},{7,3},{8,4},{9,5},{1... | collective-permute-start | bytes 270344 | tf_op jit(solution)/shard_map/ppermute | solution.py:1045
where the time goes:
time: 28.6 us; the launch traced here: 28.4 us
  Pallas kernels  11.6 us (41%)
  starting transfers between devices  9.41 us (33%)
  waiting for transfers between devices  5.9 us (21%)
  local copies, waits for them, and re-layouts  0.8 us (3%)
  between operations  0.67 us (2%)
    pallas_call x1, Pallas kernels, one_exchange(): pl.pallas_call(functools.partial(main_kernel, nz, local_z), out_shape=(ja...  9.92 us
    ppermute x6, starting transfers between devices, send(): return lax.ppermute(array, ('plane', 'thick'), route)  9.41 us
    ppermute x6, waiting for transfers between devices, send(): return lax.ppermute(array, ('plane', 'thick'), route)  5.9 us
    pallas_call x1, Pallas kernels, one_exchange(): pl.pallas_call(functools.partial(pack_kernel, nz, local_z), out_shape=(ja...  1.66 us
    unnamed x5, local copies, waits for them, and re-layouts  0.8 us
  transfers between devices with their start and end apart: 6, of which 4 were waited for; matrix products, arithmetic and copies ran while one was open for 3% of the time, Pallas kernels for 0%

commit v1 on v0

--- a/solution.py
+++ b/solution.py
@@ -300,7 +300,6 @@
 
 HALF = 128
 GROUP = 32
-EDGE = 8
 ROW_TILES = 3
 CZ = [int(v[0]) for v in VELOCITIES]
 CX = [int(v[1]) for v in VELOCITIES]
@@ -310,6 +309,10 @@
 
 def lanes():
     return lax.broadcasted_iota(jnp.int32, (8, HALF), 1)
+
+
+def places():
+    return (lanes() + GROUP // 2) & (HALF - 1)
 
 
 def rows():
@@ -354,7 +357,7 @@
         moved = layers[1:] + [zero] if dz == 1 else [zero] + layers[:-1]
         side = turn(side, -GROUP * dz)
         if fill:
-            inside = lanes() < HALF - GROUP if dz == 1 else lanes() >= GROUP
+            inside = places() < HALF - GROUP if dz == 1 else places() >= GROUP
             side = jnp.where(inside, side, 0.0)
         out.append(moved + [side])
     return out
@@ -372,52 +375,32 @@
     ]
 
 
+def y_ends(units):
+    layers, side = units[:-1], units[-1]
+    place = places()
+    beyond, ends = [], None
+    for z, tile in enumerate(layers):
+        beyond.append(turn(side, -(GROUP * z + 1)))
+        turned = turn(tile, GROUP * z + 1)
+        ends = turned if ends is None else jnp.where(place >= GROUP * z, turned, ends)
+    return beyond, ends
+
+
+def y_step(units, ready, dy):
+    beyond, ends = ready
+    at_end = lanes() == (HALF - 1 if dy == 1 else 0)
+    at_side = (places() & (GROUP - 1)) == (GROUP // 2 + 1 if dy == 1 else GROUP // 2)
+    out = [jnp.where(at_end, b, turn(t, -dy)) for t, b in zip(units, beyond)]
+    return out + [jnp.where(at_side, ends, turn(units[-1], dy))]
+
+
 def y_shift(field, dy):
-    lane = lanes()
-    out = []
-    for units in field:
-        layers, side = units[:-1], units[-1]
-        moved = []
-        if dy == 1:
-            inner = turn(side, -1)
-            for z, tile in enumerate(layers):
-                beyond = turn(side, HALF - 1 - (GROUP * z + GROUP - EDGE))
-                moved.append(jnp.where(lane == HALF - 1, beyond, turn(tile, -1)))
-                at = GROUP * z + EDGE - 1
-                inner = jnp.where(lane == at, turn(tile, at), inner)
-        else:
-            inner = turn(side, 1)
-            for z, tile in enumerate(layers):
-                beyond = turn(side, -(GROUP * z + EDGE - 1))
-                moved.append(jnp.where(lane == 0, beyond, turn(tile, 1)))
-                at = GROUP * z + GROUP - EDGE
-                inner = jnp.where(lane == at, turn(tile, at + 1), inner)
-        out.append(moved + [inner])
-    return out
+    return [y_step(units, y_ends(units), dy) for units in field]
 
 
 def y_both(field):
-    lane = lanes()
-    spot = lane & (GROUP - 1)
-    ahead, behind = [], []
-    for units in field:
-        layers, side = units[:-1], units[-1]
-        edges = None
-        up, down = [], []
-        for z, tile in enumerate(layers):
-            at = GROUP * z + EDGE - 1
-            turned = turn(tile, at)
-            edges = turned if edges is None else jnp.where(lane >= GROUP * z, turned, edges)
-            beyond = turn(side, HALF - 1 - (GROUP * z + GROUP - EDGE))
-            up.append(jnp.where(lane == HALF - 1, beyond, turn(tile, -1)))
-            beyond = turn(side, -(GROUP * z + EDGE - 1))
-            down.append(jnp.where(lane == 0, beyond, turn(tile, 1)))
-        up.append(jnp.where(spot == EDGE - 1, edges, turn(side, -1)))
-        lifted = turn(edges, GROUP - EDGE - (EDGE - 2))
-        down.append(jnp.where(spot == GROUP - EDGE, lifted, turn(side, 1)))
-        ahead.append(up)
-        behind.append(down)
-    return ahead, behind
+    ready = [y_ends(units) for units in field]
+    return tuple([y_step(u, e, dy) for u, e in zip(field, ready)] for dy in (1, -1))
 
 
 def x_both(field):
@@ -429,26 +412,33 @@
 
 
 def gradient(field):
-    ahead, behind = z_both(field)
-    two = each(lambda m, u, d: 2.0 * m + (u + d), field, ahead, behind)
-    y_sum = each(add, *y_both(field))
+    two = each(lambda m, u, d: 2.0 * m + (u + d), field, *z_both(field))
+    y_up, y_down = y_both(field)
+    y_sum, y_slope = each(add, y_up, y_down), each(sub, y_up, y_down)
     x_sum = each(add, *x_both(field))
     along_x = each(sub, *x_both(each(add, two, y_sum)))
-    along_y = each(sub, *y_both(each(add, two, x_sum)))
     flat = each(lambda m, a, b: 2.0 * m + (a + b), field, x_sum, y_sum)
     along_z = each(sub, *z_both(flat))
+    along_y = each(
+        lambda m, a, b, c, d: 2.0 * m + ((a + b) + (c + d)),
+        y_slope, *z_both(y_slope), *x_both(y_slope),
+    )
     return along_z, along_x, along_y
 
 
 def gradient_back(gz, gx, gy):
-    def around(field, first, second):
-        s = each(add, *first(field))
-        t = each(add, *second(field))
-        return each(lambda m, a, b: 2.0 * m + (a + b), field, s, t)
-
-    result = each(sub, *x_both(around(gx, z_both, y_both)))
-    result = each(add, result, each(sub, *y_both(around(gy, z_both, x_both))))
-    return each(add, result, each(sub, *z_both(around(gz, x_both, y_both))))
+    dx, dz = each(sub, *x_both(gx)), each(sub, *z_both(gz))
+    level = each(
+        lambda a, b, c, d, e, f: 2.0 * (a + b) + ((c + d) + (e + f)),
+        dx, dz, *z_both(dx), *x_both(dz),
+    )
+    across = each(add, dx, dz)
+    along = each(
+        lambda m, a, b, c, d: 2.0 * m + ((a + b) + (c + d)), gy, *z_both(gy), *x_both(gy)
+    )
+    ahead = y_shift(each(add, across, along), 1)
+    behind = y_shift(each(sub, across, along), -1)
+    return each(lambda a, b, c: a + (b + c), level, ahead, behind)
 
 
 def all_moved(field):
@@ -464,9 +454,7 @@
     return out
 
 
-def moved_by(field, dz, dx, dy):
-    if dy:
-        field = y_shift(field, dy)
+def moved_by(field, dz, dx):
     if dx:
         field = x_shift(field, dx)
     if dz:
@@ -581,9 +569,9 @@
         if 1 not in level:
             acc[k, r, u] = level[0]
         elif u == side:
-            lane = lanes()
-            up = jnp.where(lane >= GROUP, turn(level[1], GROUP), 0.0)
-            down = jnp.where(lane < HALF - GROUP, turn(level[-1], -GROUP), 0.0)
+            place = places()
+            up = jnp.where(place >= GROUP, turn(level[1], GROUP), 0.0)
+            down = jnp.where(place < HALF - GROUP, turn(level[-1], -GROUP), 0.0)
             acc[k, r, u] = level[0] + (up + down)
         else:
             acc[k, r, u] = acc[k, r, u] + level[0] if u else level[0]
@@ -627,8 +615,7 @@
     side = nz
     per = 3 * local_z + 1
     edge0 = 2 * per
-    spot = lanes() & (GROUP - 1)
-    left_part = spot < GROUP // 2
+    left_part = (places() & (GROUP - 1)) > GROUP // 2
 
     def edge(ref, k):
         if k == 3:
@@ -679,6 +666,7 @@
 
     store_gradient(g1, 0, read(p1))
     store_gradient(dg, 0, read(dp1))
+    across = {}
     for r in range(ROW_TILES):
         for u in range(units):
             dens, psi = rho[r, u], p1[r, u]
@@ -719,6 +707,10 @@
                     values += [scaled[k] + odds[k], scaled[k] - odds[k]]
                     stay += [s[2 * k + 1] * values[-2], s[2 * k + 2] * values[-1]]
                 scatter_groups(acc.at[pl.ds(first, 9)], r, u, values, total(stay))
+        for ref in (t_st, dt_st):
+            for k in range(9):
+                if CY[2 * k + 1]:
+                    across[ref is t_st, k, r] = y_both([[ref[k, r, u] for u in range(units)]])
 
     for ref, store in ((t_st, pop), (dt_st, dpop)):
         for k in range(9):
@@ -726,7 +718,8 @@
             field = read(ref.at[k])
             ahead, behind = field, field
             if CY[i]:
-                ahead, behind = y_both(field)
+                shifted = [across[ref is t_st, k, r] for r in range(ROW_TILES)]
+                ahead, behind = [[pair[j][0] for pair in shifted] for j in (0, 1)]
                 if CY[i] == -1:
                     ahead, behind = behind, ahead
             if CX[i]:
@@ -918,6 +911,7 @@
                 adj[i, r, u] = hat[i]
 
     field = gradient_back(*[read(gbar.at[k]) for k in range(3)])
+    ahead = {i: [] for i in range(1, 19)}
     for r in range(2):
         for u in range(units):
             fluid = fluid_of(rho_n[r][u])
@@ -936,9 +930,12 @@
             for k in range(9):
                 adj[2 * k + 1, r, u] = keep * adj[2 * k + 1, r, u] + (dens_bar + push[k])
                 adj[2 * k + 2, r, u] = keep * adj[2 * k + 2, r, u] + (dens_bar - push[k])
+        for i in range(1, 19):
+            tiles = [[adj[i, r, u] for u in range(units)]]
+            ahead[i] += y_shift(tiles, CY[i]) if CY[i] else tiles
 
     ahead_r = all_moved(read(adj.at[19]))
-    ahead = [None] + [moved_by(read(adj.at[i]), CZ[i], CX[i], CY[i]) for i in range(1, 19)]
+    ahead = {i: moved_by(ahead[i], CZ[i], CX[i]) for i in range(1, 19)}
     for r in range(2):
         for u in range(units):
             dens = rho_n[r][u]
@@ -979,17 +976,14 @@
                 out_ref, edge_ref):
     thick = lax.axis_index("thick")
     lane = lanes()
-    spot = lane & (GROUP - 1)
-    ends = (spot < EDGE, spot >= GROUP - EDGE)
+    place = places()
+    spot = place & (GROUP - 1)
+    source = jnp.where(spot > GROUP // 2, HALF + GROUP // 2 - spot, GROUP // 2 - spot)
     zero = jnp.zeros((8, HALF), jnp.float32)
     edges = [zero, zero, zero]
 
-    def place(tile, z, into):
-        here = (lane >= GROUP * z) & (lane < GROUP * z + GROUP)
-        last = pltpu.roll(tile, lax.rem(GROUP * z + EDGE, HALF), 1)
-        first = pltpu.roll(tile, lax.rem(GROUP * z + GROUP - EDGE, HALF), 1)
-        into = jnp.where(here & ends[0], last, into)
-        return jnp.where(here & ends[1], first, into)
+    def ends(tile):
+        return jnp.take_along_axis(tile, source, axis=1)
 
     for zl in range(local_z):
         solid = solid_ref[zl].astype(jnp.float32)
@@ -1001,22 +995,15 @@
         values = (red + blue, fluid * psi + solid * wet_ref[zl], solid * dir_ref[zl])
         for k, value in enumerate(values):
             out_ref[k * local_z + zl] = value
-            edges[k] = place(value, thick * local_z + zl, edges[k])
+            here = (place // GROUP) == thick * local_z + zl
+            edges[k] = jnp.where(here, ends(value), edges[k])
     pixels = map_ref[...]
     counts = jnp.zeros(pixels.shape, jnp.int32)
     for k in range(pixels.shape[1]):
         counts = counts + (turn(pixels, k) == lane).astype(jnp.int32)
     counts = counts.astype(jnp.float32)
     out_ref[3 * local_z] = counts
-    by_layer = zero
-    for z in range(nz):
-        by_layer = jnp.where(
-            (lane >= GROUP * z) & ends[0], turn(counts, GROUP * z + EDGE), by_layer
-        )
-        by_layer = jnp.where(
-            (lane >= GROUP * z) & ends[1], turn(counts, GROUP * z + GROUP - EDGE), by_layer
-        )
-    for k, tile in enumerate(edges + [by_layer]):
+    for k, tile in enumerate(edges + [ends(counts)]):
         edge_ref[k] = tile
 
 

time: 28.6 us -> 24.8 us (0.87)
  Pallas kernels: 11.6 us -> 7.83 us
    pallas_call x1, Pallas kernels: 9.92 us -> 6.17 us  [one_exchange(): pl.pallas_call(functools.partial(main_kernel, nz, local_z), out_shape=(ja...]
where the time goes in v1:
time: 24.8 us; the launch traced here: 24.6 us
  starting transfers between devices  9.41 us (38%)
  Pallas kernels  7.83 us (32%)
  waiting for transfers between devices  5.9 us (24%)
  local copies, waits for them, and re-layouts  0.8 us (3%)
  between operations  0.67 us (3%)
    ppermute x6, starting transfers between devices, send(): return lax.ppermute(array, ('plane', 'thick'), route)  9.41 us
    pallas_call x1, Pallas kernels, one_exchange(): pl.pallas_call(functools.partial(main_kernel, nz, local_z), out_shape=(ja...  6.17 us
    ppermute x6, waiting for transfers between devices, send(): return lax.ppermute(array, ('plane', 'thick'), route)  5.9 us
    pallas_call x1, Pallas kernels, one_exchange(): pl.pallas_call(functools.partial(pack_kernel, nz, local_z), out_shape=(ja...  1.66 us
    unnamed x5, local copies, waits for them, and re-layouts  0.8 us
  transfers between devices with their start and end apart: 6, of which 4 were waited for; matrix products, arithmetic and copies ran while one was open for 3% of the time, Pallas kernels for 0%

profile of v1, /device:TPU:0, one launch (start us, length us, event | category | flops | bytes accessed | tf_op | source)
XLA Modules:
  0.0 24.6 jit_solution(13514484709673515174)
XLA Ops:
  0.6 1.7 %shard_map.77 = (f32[7,8,128]{2,1,0:T(8,128)}, f32[4,8,128]{2,1,0:T(8,128)}) custom-call(s32[2,8,128]{2,1,0:T(8,128)} %bitcast.12, s32[2,8,128]{2,1,0:T(8,128)} %bitcast.13, f32[2,8,128]{2,1,0:T(8,128)} %bitcast.14, f32[2,8,128]{2,1,0:T(8,128)} %bitcast.15, f32[2,8,128]{2,1,0:T(8,128)} %bitcast.16, s32[8,128]{1,0:T(8,128)} %bitcast.10), custom_call_target="tpu_custom_call" | custom-call | tf_op jit(solution)/shard_map/pallas_call | solution.py:1016
  2.3 2.4 %collective-permute-start.2 = (f32[4,8,128]{2,1,0:T(8,128)}, f32[4,8,128]{2,1,0:T(8,128)S(1)}, u32[]{:S(2)}, u32[]{:S(2)}) collective-permute-start(f32[4,8,128]{2,1,0:T(8,128)} %get-tuple-element.7), channel_id=1, source_target_pairs={{0,3},{1,2},{2,1},{3,0},{4,7},{5,6},{6,5},{7,4},{8,11},{9,10},{10,... | collective-permute-start | bytes 49160 | tf_op jit(solution)/shard_map/ppermute | solution.py:1032
  4.7 0.7 %collective-permute-start.1 = (f32[4,8,128]{2,1,0:T(8,128)}, f32[4,8,128]{2,1,0:T(8,128)S(1)}, u32[]{:S(2)}, u32[]{:S(2)}) collective-permute-start(f32[4,8,128]{2,1,0:T(8,128)} %get-tuple-element.7), channel_id=1, source_target_pairs={{0,2},{1,3},{2,0},{3,1},{4,6},{5,7},{6,4},{7,5},{8,10},{9,11},{10,... | collective-permute-start | bytes 49160 | tf_op jit(solution)/shard_map/ppermute | solution.py:1032
  5.3 0.0 collective-permute-start
  5.3 0.8 %constant_dynamic-update-slice_fusion.3 = f32[22,8,128]{2,1,0:T(8,128)S(1)} fusion(f32[7,8,128]{2,1,0:T(8,128)} %get-tuple-element.6), kind=kLoop, calls=%fused_computation.3 | loop fusion | bytes 57344
  6.1 3.3 %collective-permute-done = f32[7,8,128]{2,1,0:T(8,128)S(1)} collective-permute-done((f32[7,8,128]{2,1,0:T(8,128)}, f32[7,8,128]{2,1,0:T(8,128)S(1)}, u32[]{:S(2)}, u32[]{:S(2)}) %collective-permute-start) | collective-permute-done | bytes 28704 | tf_op jit(solution)/shard_map/ppermute | solution.py:1032
  9.4 0.0 collective-permute-done.1
  9.4 0.0 copy-start
  9.4 0.0 collective-permute-done.2
  9.5 1.6 %collective-permute-start.5 = (f32[22,8,128]{2,1,0:T(8,128)S(1)}, f32[22,8,128]{2,1,0:T(8,128)S(1)}, u32[]{:S(2)}, u32[]{:S(2)}) collective-permute-start(f32[22,8,128]{2,1,0:T(8,128)S(1)} %constant_dynamic-update-slice_fusion.q_ref), channel_id=1, source_target_pairs={{0,4},{1,5},{2,6},{3,7},{4,8},{5,9},{6,10},{7,11},{8,12},{9,13},{1... | collective-permute-start | bytes 270344 | tf_op jit(solution)/shard_map/ppermute | solution.py:1032
  11.0 1.6 %collective-permute-start.4 = (f32[22,8,128]{2,1,0:T(8,128)S(1)}, f32[22,8,128]{2,1,0:T(8,128)S(1)}, u32[]{:S(2)}, u32[]{:S(2)}) collective-permute-start(f32[22,8,128]{2,1,0:T(8,128)S(1)} %constant_dynamic-update-slice_fusion.q_ref), channel_id=1, source_target_pairs={{0,8},{1,9},{2,26},{3,27},{4,12},{5,13},{6,30},{7,31},{8,16},{9,17... | collective-permute-start | bytes 270344 | tf_op jit(solution)/shard_map/ppermute | solution.py:1032
  12.6 3.2 %collective-permute-start.3 = (f32[22,8,128]{2,1,0:T(8,128)S(1)}, f32[22,8,128]{2,1,0:T(8,128)S(1)}, u32[]{:S(2)}, u32[]{:S(2)}) collective-permute-start(f32[22,8,128]{2,1,0:T(8,128)S(1)} %constant_dynamic-update-slice_fusion.q_ref), channel_id=1, source_target_pairs={{0,28},{1,29},{2,30},{3,31},{4,0},{5,1},{6,2},{7,3},{8,4},{9,5},{1... | collective-permute-start | bytes 270344 | tf_op jit(solution)/shard_map/ppermute | solution.py:1032
  15.8 1.4 %collective-permute-done.5.qm_ref = f32[22,8,128]{2,1,0:T(8,128)S(1)} collective-permute-done((f32[22,8,128]{2,1,0:T(8,128)S(1)}, f32[22,8,128]{2,1,0:T(8,128)S(1)}, u32[]{:S(2)}, u32[]{:S(2)}) %collective-permute-start.5) | collective-permute-done | bytes 90144 | tf_op jit(solution)/shard_map/ppermute | solution.py:1032
  17.2 0.2 collective-permute-done.4.sl_ref
  17.4 1.0 %collective-permute-done.3.qp_ref = f32[22,8,128]{2,1,0:T(8,128)S(1)} collective-permute-done((f32[22,8,128]{2,1,0:T(8,128)S(1)}, f32[22,8,128]{2,1,0:T(8,128)S(1)}, u32[]{:S(2)}, u32[]{:S(2)}) %collective-permute-start.3) | collective-permute-done | bytes 90144 | tf_op jit(solution)/shard_map/ppermute | solution.py:1032
  18.4 0.0 copy-done
  18.4 6.2 %shard_map.78 = (f32[2,8,128]{2,1,0:T(8,128)}, f32[8,128]{1,0:T(8,128)}) custom-call(f32[22,8,128]{2,1,0:T(8,128)S(1)} %collective-permute-done.3.qp_ref, f32[22,8,128]{2,1,0:T(8,128)S(1)} %collective-permute-done.4.sl_ref, f32[22,8,128]{2,1,0:T(8,128)S(1)} %collective-permute-done.5.qm_ref, f32[22,8,128]{2,1,0:T(8,128)S(1)} %constant_dynamic-update-slice_fusion.q_ref, ...), custom_call_target="tpu_custom_call" | custom-call | tf_op jit(solution)/shard_map/pallas_call | solution.py:1045
  (3 shorter events, 0.0 us)
Async XLA Ops:
  2.3 7.2 %collective-permute-start.2 = (f32[4,8,128]{2,1,0:T(8,128)}, f32[4,8,128]{2,1,0:T(8,128)S(1)}, u32[]{:S(2)}, u32[]{:S(2)}) collective-permute-start(f32[4,8,128]{2,1,0:T(8,128)} %get-tuple-element.7), channel_id=1, source_target_pairs={{0,3},{1,2},{2,1},{3,0},{4,7},{5,6},{6,5},{7,4},{8,11},{9,10},{10,... | collective-permute-start | bytes 49160 | tf_op jit(solution)/shard_map/ppermute | solution.py:1032
  4.7 4.8 %collective-permute-start.1 = (f32[4,8,128]{2,1,0:T(8,128)}, f32[4,8,128]{2,1,0:T(8,128)S(1)}, u32[]{:S(2)}, u32[]{:S(2)}) collective-permute-start(f32[4,8,128]{2,1,0:T(8,128)} %get-tuple-element.7), channel_id=1, source_target_pairs={{0,2},{1,3},{2,0},{3,1},{4,6},{5,7},{6,4},{7,5},{8,10},{9,11},{10,... | collective-permute-start | bytes 49160 | tf_op jit(solution)/shard_map/ppermute | solution.py:1032
  5.3 4.1 %collective-permute-start = (f32[7,8,128]{2,1,0:T(8,128)}, f32[7,8,128]{2,1,0:T(8,128)S(1)}, u32[]{:S(2)}, u32[]{:S(2)}) collective-permute-start(f32[7,8,128]{2,1,0:T(8,128)} %get-tuple-element.6), channel_id=1, source_target_pairs={{0,1},{1,0},{2,3},{3,2},{4,5},{5,4},{6,7},{7,6},{8,9},{9,8},{10,11... | collective-permute-start | bytes 86024 | tf_op jit(solution)/shard_map/ppermute | solution.py:1032
  9.4 9.0 %copy-start = (s32[1,8,128]{2,1,0:T(8,128)S(1)}, s32[1,8,128]{2,1,0:T(8,128)}, u32[]{:S(2)}) copy-start(s32[1,8,128]{2,1,0:T(8,128)} %param.11) | copy-start | bytes 12292
  9.5 7.7 %collective-permute-start.5 = (f32[22,8,128]{2,1,0:T(8,128)S(1)}, f32[22,8,128]{2,1,0:T(8,128)S(1)}, u32[]{:S(2)}, u32[]{:S(2)}) collective-permute-start(f32[22,8,128]{2,1,0:T(8,128)S(1)} %constant_dynamic-update-slice_fusion.q_ref), channel_id=1, source_target_pairs={{0,4},{1,5},{2,6},{3,7},{4,8},{5,9},{6,10},{7,11},{8,12},{9,13},{1... | collective-permute-start | bytes 270344 | tf_op jit(solution)/shard_map/ppermute | solution.py:1032
  11.0 6.3 %collective-permute-start.4 = (f32[22,8,128]{2,1,0:T(8,128)S(1)}, f32[22,8,128]{2,1,0:T(8,128)S(1)}, u32[]{:S(2)}, u32[]{:S(2)}) collective-permute-start(f32[22,8,128]{2,1,0:T(8,128)S(1)} %constant_dynamic-update-slice_fusion.q_ref), channel_id=1, source_target_pairs={{0,8},{1,9},{2,26},{3,27},{4,12},{5,13},{6,30},{7,31},{8,16},{9,17... | collective-permute-start | bytes 270344 | tf_op jit(solution)/shard_map/ppermute | solution.py:1032
  12.6 5.8 %collective-permute-start.3 = (f32[22,8,128]{2,1,0:T(8,128)S(1)}, f32[22,8,128]{2,1,0:T(8,128)S(1)}, u32[]{:S(2)}, u32[]{:S(2)}) collective-permute-start(f32[22,8,128]{2,1,0:T(8,128)S(1)} %constant_dynamic-update-slice_fusion.q_ref), channel_id=1, source_target_pairs={{0,28},{1,29},{2,30},{3,31},{4,0},{5,1},{6,2},{7,3},{8,4},{9,5},{1... | collective-permute-start | bytes 270344 | tf_op jit(solution)/shard_map/ppermute | solution.py:1032

commit v2 on v1

--- a/solution.py
+++ b/solution.py
@@ -301,6 +301,7 @@
 HALF = 128
 GROUP = 32
 ROW_TILES = 3
+ROW_SLOTS = 120
 CZ = [int(v[0]) for v in VELOCITIES]
 CX = [int(v[1]) for v in VELOCITIES]
 CY = [int(v[2]) for v in VELOCITIES]
@@ -363,16 +364,39 @@
     return out
 
 
+class RowSpace:
+    ref, used = None, 0
+
+    @classmethod
+    def start(cls, ref):
+        cls.ref, cls.used = ref, 0
+
+    @classmethod
+    def put(cls, field):
+        slot, cls.used = cls.used, cls.used + 1
+        if len(field) == ROW_TILES:
+            order = (2, 0, 1)
+        else:
+            order = (1, 0, 1)
+        for u in range(len(field[0])):
+            for k, r in enumerate(order):
+                cls.ref[slot, u, 8 * (k + 1) : 8 * (k + 2), :] = field[r][u]
+        return slot
+
+    @classmethod
+    def get(cls, slot, count, units, dx):
+        if count == ROW_TILES:
+            order = (2, 3, 1)
+        else:
+            order = (2, 1 if dx == 1 else 3)
+        return [
+            [cls.ref[slot, u, 8 * k + dx : 8 * (k + 1) + dx, :] for u in range(units)]
+            for k in order
+        ]
+
+
 def x_shift(field, dx):
-    count = len(field)
-    at_edge = rows() == (0 if dx == 1 else 7)
-    return [
-        [
-            pltpu.roll(jnp.where(at_edge, beyond, here), (-dx) % 8, 0)
-            for here, beyond in zip(field[r], field[(r + dx) % count])
-        ]
-        for r in range(count)
-    ]
+    return RowSpace.get(RowSpace.put(field), len(field), len(field[0]), dx)
 
 
 def y_ends(units):
@@ -404,7 +428,8 @@
 
 
 def x_both(field):
-    return x_shift(field, 1), x_shift(field, -1)
+    slot = RowSpace.put(field)
+    return tuple(RowSpace.get(slot, len(field), len(field[0]), dx) for dx in (1, -1))
 
 
 def z_both(field):
@@ -608,7 +633,8 @@
 
 def main_kernel(nz, local_z, qp_ref, sl_ref, qm_ref, q_ref, map_ref, out_ref, read_ref,
                 rho, p1, dp1, blk, t_st, dt_st, acc, pop, dpop, mac, p2, dp2, g1, g2, dg,
-                a3, b3, adj, gbar, pbar2):
+                a3, b3, adj, gbar, pbar2, row_space):
+    RowSpace.start(row_space)
     thick = lax.axis_index("thick")
     even = lax.rem(lax.axis_index("plane"), 2) == 0
     units = nz + 1
@@ -1055,8 +1081,9 @@
             field(19), field(19), field(6), field(), field(), field(3), field(3), field(3),
             field(tiles=2), field(tiles=2), field(24, tiles=2), field(3, tiles=2),
             pltpu.VMEM((nz, 8, HALF), jnp.float32),
+            pltpu.VMEM((ROW_SLOTS, nz + 1, 8 * (ROW_TILES + 2), HALF), jnp.float32),
         ],
-        compiler_params=pltpu.CompilerParams(vmem_limit_bytes=24 * 1024 * 1024),
+        compiler_params=pltpu.CompilerParams(vmem_limit_bytes=32 * 1024 * 1024),
     )(below, corner, above, quad, pixel_map[0])
 
 

time: 24.8 us -> 24.5 us (0.988)
  Pallas kernels: 7.83 us -> 7.49 us
    pallas_call x1, Pallas kernels: 6.17 us -> 5.84 us  [one_exchange(): pl.pallas_call(functools.partial(main_kernel, nz, local_z), out_shape=(ja...]
where the time goes in v2:
time: 24.5 us; the launch traced here: 24.3 us
  starting transfers between devices  9.41 us (38%)
  Pallas kernels  7.49 us (31%)
  waiting for transfers between devices  5.9 us (24%)
  local copies, waits for them, and re-layouts  0.8 us (3%)
  between operations  0.67 us (3%)
    ppermute x6, starting transfers between devices, send(): return lax.ppermute(array, ('plane', 'thick'), route)  9.41 us
    ppermute x6, waiting for transfers between devices, send(): return lax.ppermute(array, ('plane', 'thick'), route)  5.9 us
    pallas_call x1, Pallas kernels, one_exchange(): pl.pallas_call(functools.partial(main_kernel, nz, local_z), out_shape=(ja...  5.84 us
    pallas_call x1, Pallas kernels, one_exchange(): pl.pallas_call(functools.partial(pack_kernel, nz, local_z), out_shape=(ja...  1.66 us
    unnamed x5, local copies, waits for them, and re-layouts  0.8 us
  transfers between devices with their start and end apart: 6, of which 4 were waited for; matrix products, arithmetic and copies ran while one was open for 3% of the time, Pallas kernels for 0%

profile of v2, /device:TPU:0, one launch (start us, length us, event | category | flops | bytes accessed | tf_op | source)
XLA Modules:
  0.0 24.3 jit_solution(18383586177527715559)
XLA Ops:
  0.6 1.7 %shard_map.77 = (f32[7,8,128]{2,1,0:T(8,128)}, f32[4,8,128]{2,1,0:T(8,128)}) custom-call(s32[2,8,128]{2,1,0:T(8,128)} %bitcast.12, s32[2,8,128]{2,1,0:T(8,128)} %bitcast.13, f32[2,8,128]{2,1,0:T(8,128)} %bitcast.14, f32[2,8,128]{2,1,0:T(8,128)} %bitcast.15, f32[2,8,128]{2,1,0:T(8,128)} %bitcast.16, s32[8,128]{1,0:T(8,128)} %bitcast.10), custom_call_target="tpu_custom_call" | custom-call | tf_op jit(solution)/shard_map/pallas_call | solution.py:1042
  2.3 2.4 %collective-permute-start.2 = (f32[4,8,128]{2,1,0:T(8,128)}, f32[4,8,128]{2,1,0:T(8,128)S(1)}, u32[]{:S(2)}, u32[]{:S(2)}) collective-permute-start(f32[4,8,128]{2,1,0:T(8,128)} %get-tuple-element.7), channel_id=1, source_target_pairs={{0,3},{1,2},{2,1},{3,0},{4,7},{5,6},{6,5},{7,4},{8,11},{9,10},{10,... | collective-permute-start | bytes 49160 | tf_op jit(solution)/shard_map/ppermute | solution.py:1058
  4.7 0.7 %collective-permute-start.1 = (f32[4,8,128]{2,1,0:T(8,128)}, f32[4,8,128]{2,1,0:T(8,128)S(1)}, u32[]{:S(2)}, u32[]{:S(2)}) collective-permute-start(f32[4,8,128]{2,1,0:T(8,128)} %get-tuple-element.7), channel_id=1, source_target_pairs={{0,2},{1,3},{2,0},{3,1},{4,6},{5,7},{6,4},{7,5},{8,10},{9,11},{10,... | collective-permute-start | bytes 49160 | tf_op jit(solution)/shard_map/ppermute | solution.py:1058
  5.3 0.0 collective-permute-start
  5.3 0.8 %constant_dynamic-update-slice_fusion.3 = f32[22,8,128]{2,1,0:T(8,128)S(1)} fusion(f32[7,8,128]{2,1,0:T(8,128)} %get-tuple-element.6), kind=kLoop, calls=%fused_computation.3 | loop fusion | bytes 57344
  6.1 3.3 %collective-permute-done = f32[7,8,128]{2,1,0:T(8,128)S(1)} collective-permute-done((f32[7,8,128]{2,1,0:T(8,128)}, f32[7,8,128]{2,1,0:T(8,128)S(1)}, u32[]{:S(2)}, u32[]{:S(2)}) %collective-permute-start) | collective-permute-done | bytes 28704 | tf_op jit(solution)/shard_map/ppermute | solution.py:1058
  9.4 0.0 collective-permute-done.1
  9.4 0.0 copy-start
  9.4 0.0 collective-permute-done.2
  9.5 1.6 %collective-permute-start.5 = (f32[22,8,128]{2,1,0:T(8,128)S(1)}, f32[22,8,128]{2,1,0:T(8,128)S(1)}, u32[]{:S(2)}, u32[]{:S(2)}) collective-permute-start(f32[22,8,128]{2,1,0:T(8,128)S(1)} %constant_dynamic-update-slice_fusion.q_ref), channel_id=1, source_target_pairs={{0,4},{1,5},{2,6},{3,7},{4,8},{5,9},{6,10},{7,11},{8,12},{9,13},{1... | collective-permute-start | bytes 270344 | tf_op jit(solution)/shard_map/ppermute | solution.py:1058
  11.0 1.6 %collective-permute-start.4 = (f32[22,8,128]{2,1,0:T(8,128)S(1)}, f32[22,8,128]{2,1,0:T(8,128)S(1)}, u32[]{:S(2)}, u32[]{:S(2)}) collective-permute-start(f32[22,8,128]{2,1,0:T(8,128)S(1)} %constant_dynamic-update-slice_fusion.q_ref), channel_id=1, source_target_pairs={{0,8},{1,9},{2,26},{3,27},{4,12},{5,13},{6,30},{7,31},{8,16},{9,17... | collective-permute-start | bytes 270344 | tf_op jit(solution)/shard_map/ppermute | solution.py:1058
  12.6 3.2 %collective-permute-start.3 = (f32[22,8,128]{2,1,0:T(8,128)S(1)}, f32[22,8,128]{2,1,0:T(8,128)S(1)}, u32[]{:S(2)}, u32[]{:S(2)}) collective-permute-start(f32[22,8,128]{2,1,0:T(8,128)S(1)} %constant_dynamic-update-slice_fusion.q_ref), channel_id=1, source_target_pairs={{0,28},{1,29},{2,30},{3,31},{4,0},{5,1},{6,2},{7,3},{8,4},{9,5},{1... | collective-permute-start | bytes 270344 | tf_op jit(solution)/shard_map/ppermute | solution.py:1058
  15.8 1.4 %collective-permute-done.5.qm_ref = f32[22,8,128]{2,1,0:T(8,128)S(1)} collective-permute-done((f32[22,8,128]{2,1,0:T(8,128)S(1)}, f32[22,8,128]{2,1,0:T(8,128)S(1)}, u32[]{:S(2)}, u32[]{:S(2)}) %collective-permute-start.5) | collective-permute-done | bytes 90144 | tf_op jit(solution)/shard_map/ppermute | solution.py:1058
  17.2 0.2 collective-permute-done.4.sl_ref
  17.4 1.0 %collective-permute-done.3.qp_ref = f32[22,8,128]{2,1,0:T(8,128)S(1)} collective-permute-done((f32[22,8,128]{2,1,0:T(8,128)S(1)}, f32[22,8,128]{2,1,0:T(8,128)S(1)}, u32[]{:S(2)}, u32[]{:S(2)}) %collective-permute-start.3) | collective-permute-done | bytes 90144 | tf_op jit(solution)/shard_map/ppermute | solution.py:1058
  18.4 0.0 copy-done
  18.4 5.8 %shard_map.78 = (f32[2,8,128]{2,1,0:T(8,128)}, f32[8,128]{1,0:T(8,128)}) custom-call(f32[22,8,128]{2,1,0:T(8,128)S(1)} %collective-permute-done.3.qp_ref, f32[22,8,128]{2,1,0:T(8,128)S(1)} %collective-permute-done.4.sl_ref, f32[22,8,128]{2,1,0:T(8,128)S(1)} %collective-permute-done.5.qm_ref, f32[22,8,128]{2,1,0:T(8,128)S(1)} %constant_dynamic-update-slice_fusion.q_ref, ...), custom_call_target="tpu_custom_call" | custom-call | tf_op jit(solution)/shard_map/pallas_call | solution.py:1071
  (3 shorter events, 0.0 us)
Async XLA Ops:
  2.3 7.2 %collective-permute-start.2 = (f32[4,8,128]{2,1,0:T(8,128)}, f32[4,8,128]{2,1,0:T(8,128)S(1)}, u32[]{:S(2)}, u32[]{:S(2)}) collective-permute-start(f32[4,8,128]{2,1,0:T(8,128)} %get-tuple-element.7), channel_id=1, source_target_pairs={{0,3},{1,2},{2,1},{3,0},{4,7},{5,6},{6,5},{7,4},{8,11},{9,10},{10,... | collective-permute-start | bytes 49160 | tf_op jit(solution)/shard_map/ppermute | solution.py:1058
  4.7 4.8 %collective-permute-start.1 = (f32[4,8,128]{2,1,0:T(8,128)}, f32[4,8,128]{2,1,0:T(8,128)S(1)}, u32[]{:S(2)}, u32[]{:S(2)}) collective-permute-start(f32[4,8,128]{2,1,0:T(8,128)} %get-tuple-element.7), channel_id=1, source_target_pairs={{0,2},{1,3},{2,0},{3,1},{4,6},{5,7},{6,4},{7,5},{8,10},{9,11},{10,... | collective-permute-start | bytes 49160 | tf_op jit(solution)/shard_map/ppermute | solution.py:1058
  5.3 4.1 %collective-permute-start = (f32[7,8,128]{2,1,0:T(8,128)}, f32[7,8,128]{2,1,0:T(8,128)S(1)}, u32[]{:S(2)}, u32[]{:S(2)}) collective-permute-start(f32[7,8,128]{2,1,0:T(8,128)} %get-tuple-element.6), channel_id=1, source_target_pairs={{0,1},{1,0},{2,3},{3,2},{4,5},{5,4},{6,7},{7,6},{8,9},{9,8},{10,11... | collective-permute-start | bytes 86024 | tf_op jit(solution)/shard_map/ppermute | solution.py:1058
  9.4 9.0 %copy-start = (s32[1,8,128]{2,1,0:T(8,128)S(1)}, s32[1,8,128]{2,1,0:T(8,128)}, u32[]{:S(2)}) copy-start(s32[1,8,128]{2,1,0:T(8,128)} %param.11) | copy-start | bytes 12292
  9.5 7.7 %collective-permute-start.5 = (f32[22,8,128]{2,1,0:T(8,128)S(1)}, f32[22,8,128]{2,1,0:T(8,128)S(1)}, u32[]{:S(2)}, u32[]{:S(2)}) collective-permute-start(f32[22,8,128]{2,1,0:T(8,128)S(1)} %constant_dynamic-update-slice_fusion.q_ref), channel_id=1, source_target_pairs={{0,4},{1,5},{2,6},{3,7},{4,8},{5,9},{6,10},{7,11},{8,12},{9,13},{1... | collective-permute-start | bytes 270344 | tf_op jit(solution)/shard_map/ppermute | solution.py:1058
  11.0 6.3 %collective-permute-start.4 = (f32[22,8,128]{2,1,0:T(8,128)S(1)}, f32[22,8,128]{2,1,0:T(8,128)S(1)}, u32[]{:S(2)}, u32[]{:S(2)}) collective-permute-start(f32[22,8,128]{2,1,0:T(8,128)S(1)} %constant_dynamic-update-slice_fusion.q_ref), channel_id=1, source_target_pairs={{0,8},{1,9},{2,26},{3,27},{4,12},{5,13},{6,30},{7,31},{8,16},{9,17... | collective-permute-start | bytes 270344 | tf_op jit(solution)/shard_map/ppermute | solution.py:1058
  12.6 5.8 %collective-permute-start.3 = (f32[22,8,128]{2,1,0:T(8,128)S(1)}, f32[22,8,128]{2,1,0:T(8,128)S(1)}, u32[]{:S(2)}, u32[]{:S(2)}) collective-permute-start(f32[22,8,128]{2,1,0:T(8,128)S(1)} %constant_dynamic-update-slice_fusion.q_ref), channel_id=1, source_target_pairs={{0,28},{1,29},{2,30},{3,31},{4,0},{5,1},{6,2},{7,3},{8,4},{9,5},{1... | collective-permute-start | bytes 270344 | tf_op jit(solution)/shard_map/ppermute | solution.py:1058

commit v3 on v2

--- a/solution.py
+++ b/solution.py
@@ -639,7 +639,7 @@
     even = lax.rem(lax.axis_index("plane"), 2) == 0
     units = nz + 1
     side = nz
-    per = 3 * local_z + 1
+    per = 3 * local_z
     edge0 = 2 * per
     left_part = (places() & (GROUP - 1)) > GROUP // 2
 
@@ -667,7 +667,7 @@
                 start = jnp.where(thick == slab, 0, per)
                 ref[r, z] = source[start + which * local_z + zl]
             ref[r, side] = beside(r, which)
-        counts.append([source[per - 1], beside(r, 3)])
+        counts.append([source[edge0 + 8], beside(r, 3)])
     counts = narrow(counts)
 
     fluid_field = each(fluid_of, read(rho))
@@ -998,56 +998,54 @@
         out_ref[zl] = chosen
 
 
-def pack_kernel(nz, local_z, solid_ref, labels_ref, density_ref, wet_ref, dir_ref, map_ref,
-                out_ref, edge_ref):
+def edge_kernel(local_z, values_ref, map_ref, edge_ref, count_ref):
     thick = lax.axis_index("thick")
     lane = lanes()
     place = places()
     spot = place & (GROUP - 1)
     source = jnp.where(spot > GROUP // 2, HALF + GROUP // 2 - spot, GROUP // 2 - spot)
-    zero = jnp.zeros((8, HALF), jnp.float32)
-    edges = [zero, zero, zero]
 
     def ends(tile):
         return jnp.take_along_axis(tile, source, axis=1)
 
-    for zl in range(local_z):
-        solid = solid_ref[zl].astype(jnp.float32)
-        label = labels_ref[zl].astype(jnp.float32)
-        fluid = 1.0 - solid
-        red = density_ref[zl] * label * fluid
-        blue = density_ref[zl] * (1.0 - label) * fluid
-        psi = (red - blue) / (red + blue + solid)
-        values = (red + blue, fluid * psi + solid * wet_ref[zl], solid * dir_ref[zl])
-        for k, value in enumerate(values):
-            out_ref[k * local_z + zl] = value
+    for k in range(3):
+        edges = jnp.zeros((8, HALF), jnp.float32)
+        for zl in range(local_z):
             here = (place // GROUP) == thick * local_z + zl
-            edges[k] = jnp.where(here, ends(value), edges[k])
+            edges = jnp.where(here, ends(values_ref[k * local_z + zl]), edges)
+        edge_ref[k] = edges
     pixels = map_ref[...]
     counts = jnp.zeros(pixels.shape, jnp.int32)
     for k in range(pixels.shape[1]):
         counts = counts + (turn(pixels, k) == lane).astype(jnp.int32)
     counts = counts.astype(jnp.float32)
-    out_ref[3 * local_z] = counts
-    for k, tile in enumerate(edges + [ends(counts)]):
-        edge_ref[k] = tile
+    edge_ref[3] = ends(counts)
+    count_ref[0] = counts
 
 
 def one_exchange(solid, labels, density, wettability, direction, pixel_map):
     local_z = solid.shape[0]
     planes, slabs = lax.axis_size("plane"), lax.axis_size("thick")
     nz = local_z * slabs
-    per = 3 * local_z + 1
     vmem = pl.BlockSpec(memory_space=pltpu.VMEM)
-    packed, edges = pl.pallas_call(
-        functools.partial(pack_kernel, nz, local_z),
+    solid_cell, label = solid[:, 0].astype(jnp.float32), labels[:, 0].astype(jnp.float32)
+    fluid = 1.0 - solid_cell
+    red = density[:, 0] * label * fluid
+    blue = density[:, 0] * (1.0 - label) * fluid
+    psi = (red - blue) / (red + blue + solid_cell)
+    packed = jnp.concatenate(
+        [red + blue, fluid * psi + solid_cell * wettability[:, 0], solid_cell * direction[:, 0]]
+    )
+    edges, counts = pl.pallas_call(
+        functools.partial(edge_kernel, local_z),
         out_shape=(
-            jax.ShapeDtypeStruct((per, 8, HALF), jnp.float32),
             jax.ShapeDtypeStruct((4, 8, HALF), jnp.float32),
+            jax.ShapeDtypeStruct((1, 8, HALF), jnp.float32),
         ),
-        in_specs=[vmem] * 6,
+        in_specs=[vmem] * 2,
         out_specs=(vmem, vmem),
-    )(solid[:, 0], labels[:, 0], density[:, 0], wettability[:, 0], direction[:, 0], pixel_map[0])
+        compiler_params=pltpu.CompilerParams(vmem_limit_bytes=1024 * 1024),
+    )(packed, pixel_map[0])
 
     def send(array, target):
         route = []
@@ -1060,7 +1058,7 @@
     beside_z = send(packed, lambda b, t: (b, 1 - t))
     beside_y = send(edges, lambda b, t: (b ^ 1, t))
     beside_zy = send(edges, lambda b, t: (b ^ 1, 1 - t))
-    quad = jnp.concatenate([packed, beside_z, beside_y, beside_zy])
+    quad = jnp.concatenate([packed, beside_z, beside_y, beside_zy, counts])
     above = send(quad, lambda b, t: (b + 2, t))
     below = send(quad, lambda b, t: (b - 2, t))
     corner = send(quad, lambda b, t: (b + 4 if b % 2 == 0 else b - 4, t))

time: 24.5 us -> 23.9 us (0.976)
  Pallas kernels: 7.49 us -> 6.1 us
  other arithmetic: 0 us -> 0.78 us
  waiting for transfers between devices: 5.9 us -> 5.27 us
  starting transfers between devices: 9.41 us -> 10 us
    pallas_call x1, Pallas kernels: 1.66 us -> 0.27 us  [one_exchange(): pl.pallas_call(functools.partial(edge_kernel, local_z), out_shape=(jax.Sh...]
    unnamed x0 -> x3, other arithmetic: none -> 0.78 us
    ppermute x6, waiting for transfers between devices: 5.9 us -> 5.27 us  [send(): return lax.ppermute(array, ('plane', 'thick'), route)]
    ppermute x6, starting transfers between devices: 9.41 us -> 10 us  [send(): return lax.ppermute(array, ('plane', 'thick'), route)]
    unnamed x5 -> x15, local copies, waits for them, and re-layouts: 0.8 us -> 0.7 us
  transfers between devices with their start and end apart: 6 -> 6, of which waited for: 4 -> 5; matrix products, arithmetic and copies ran while one was open for 3% -> 0% of each run, Pallas kernels for 0% -> 1%
where the time goes in v3:
time: 23.9 us; the launch traced here: 23.6 us
  starting transfers between devices  10 us (42%)
  Pallas kernels  6.1 us (26%)
  waiting for transfers between devices  5.27 us (22%)
  other arithmetic  0.78 us (3%)
  between operations  0.72 us (3%)
  local copies, waits for them, and re-layouts  0.7 us (3%)
    ppermute x6, starting transfers between devices, send(): return lax.ppermute(array, ('plane', 'thick'), route)  10 us
    pallas_call x1, Pallas kernels, one_exchange(): pl.pallas_call(functools.partial(main_kernel, nz, local_z), out_shape=(ja...  5.83 us
    ppermute x6, waiting for transfers between devices, send(): return lax.ppermute(array, ('plane', 'thick'), route)  5.27 us
    unnamed x3, other arithmetic  0.78 us
    unnamed x15, local copies, waits for them, and re-layouts  0.7 us
  transfers between devices with their start and end apart: 6, of which 5 were waited for; matrix products, arithmetic and copies ran while one was open for 0% of the time, Pallas kernels for 1%

profile of v3, /device:TPU:0, one launch (start us, length us, event | category | flops | bytes accessed | tf_op | source)
XLA Modules:
  0.0 23.6 jit_solution(16475429104079046061)
XLA Ops:
  0.6 0.0 copy-start.1
  0.6 0.0 copy-start.2
  0.7 0.0 copy-start.3
  0.7 0.0 copy-start.4
  0.7 0.8 %constant_dynamic-update-slice_fusion.6 = (f32[21,8,128]{2,1,0:T(8,128)S(1)}, f32[2,8,128]{2,1,0:T(8,128)S(1)}) fusion(s32[2,1,8,128]{3,2,1,0:T(8,128)} %param.6, s32[2,1,8,128]{3,2,1,0:T(8,128)} %param.7, f32[2,1,8,128]{3,2,1,0:T(8,128)} %param.8), kind=kLoop, calls=%fused_computation.7 | loop fusion | flops 18431 | bytes 40960
  1.4 0.0 copy-done.1
  1.4 0.0 copy-done.2
  1.4 0.0 copy-done.3
  1.5 0.0 copy-done.4
  1.5 0.0 copy-start.5
  1.5 0.7 %copy-done.5 = f32[2,1,8,128]{3,2,1,0:T(8,128)S(1)} copy-done((f32[2,1,8,128]{3,2,1,0:T(8,128)S(1)}, f32[2,1,8,128]{3,2,1,0:T(8,128)}, u32[]{:S(2)}) %copy-start.5) | copy-done | bytes 8216
  2.2 0.0 copy-start
  2.2 3.0 %collective-permute-start = (f32[6,8,128]{2,1,0:T(8,128)S(1)}, f32[6,8,128]{2,1,0:T(8,128)S(1)}, u32[]{:S(2)}, u32[]{:S(2)}) collective-permute-start(f32[6,8,128]{2,1,0:T(8,128)S(1)} %pad_maximum_fusion.values_ref), channel_id=1, source_target_pairs={{0,1},{1,0},{2,3},{3,2},{4,5},{5,4},{6,7},{7,6},{8,9},{9,8},{10,11... | collective-permute-start | bytes 73736 | tf_op jit(solution)/shard_map/ppermute | solution.py:1056
  5.2 0.0 copy-done
  5.2 0.3 %shard_map.77 = (f32[4,8,128]{2,1,0:T(8,128)S(1)}, f32[1,8,128]{2,1,0:T(8,128)S(1)}) custom-call(f32[6,8,128]{2,1,0:T(8,128)S(1)} %pad_maximum_fusion.values_ref, s32[8,128]{1,0:T(8,128)S(1)} %bitcast.114), custom_call_target="tpu_custom_call" | custom-call | tf_op jit(solution)/shard_map/pallas_call | solution.py:1039
  5.5 0.1 collective-permute-start.2
  5.5 0.7 %collective-permute-start.1 = (f32[4,8,128]{2,1,0:T(8,128)S(1)}, f32[4,8,128]{2,1,0:T(8,128)S(1)}, u32[]{:S(2)}, u32[]{:S(2)}) collective-permute-start(f32[4,8,128]{2,1,0:T(8,128)S(1)} %get-tuple-element.6), channel_id=1, source_target_pairs={{0,2},{1,3},{2,0},{3,1},{4,6},{5,7},{6,4},{7,5},{8,10},{9,11},{10,... | collective-permute-start | bytes 49160 | tf_op jit(solution)/shard_map/ppermute | solution.py:1056
  6.2 0.8 %collective-permute-done = f32[6,8,128]{2,1,0:T(8,128)S(1)} collective-permute-done((f32[6,8,128]{2,1,0:T(8,128)S(1)}, f32[6,8,128]{2,1,0:T(8,128)S(1)}, u32[]{:S(2)}, u32[]{:S(2)}) %collective-permute-start) | collective-permute-done | bytes 24608 | tf_op jit(solution)/shard_map/ppermute | solution.py:1056
  7.0 0.0 collective-permute-done.1
  7.0 1.6 %collective-permute-done.2 = f32[4,8,128]{2,1,0:T(8,128)S(1)} collective-permute-done((f32[4,8,128]{2,1,0:T(8,128)S(1)}, f32[4,8,128]{2,1,0:T(8,128)S(1)}, u32[]{:S(2)}, u32[]{:S(2)}) %collective-permute-start.2) | collective-permute-done | bytes 16416 | tf_op jit(solution)/shard_map/ppermute | solution.py:1056
  8.6 1.5 %collective-permute-start.5 = (f32[21,8,128]{2,1,0:T(8,128)S(1)}, f32[21,8,128]{2,1,0:T(8,128)S(1)}, u32[]{:S(2)}, u32[]{:S(2)}) collective-permute-start(f32[21,8,128]{2,1,0:T(8,128)S(1)} %constant_dynamic-update-slice_fusion.q_ref), channel_id=1, source_target_pairs={{0,4},{1,5},{2,6},{3,7},{4,8},{5,9},{6,10},{7,11},{8,12},{9,13},{1... | collective-permute-start | bytes 258056 | tf_op jit(solution)/shard_map/ppermute | solution.py:1056
  10.2 1.6 %collective-permute-start.4 = (f32[21,8,128]{2,1,0:T(8,128)S(1)}, f32[21,8,128]{2,1,0:T(8,128)S(1)}, u32[]{:S(2)}, u32[]{:S(2)}) collective-permute-start(f32[21,8,128]{2,1,0:T(8,128)S(1)} %constant_dynamic-update-slice_fusion.q_ref), channel_id=1, source_target_pairs={{0,8},{1,9},{2,26},{3,27},{4,12},{5,13},{6,30},{7,31},{8,16},{9,17... | collective-permute-start | bytes 258056 | tf_op jit(solution)/shard_map/ppermute | solution.py:1056
  11.7 3.2 %collective-permute-start.3 = (f32[21,8,128]{2,1,0:T(8,128)S(1)}, f32[21,8,128]{2,1,0:T(8,128)S(1)}, u32[]{:S(2)}, u32[]{:S(2)}) collective-permute-start(f32[21,8,128]{2,1,0:T(8,128)S(1)} %constant_dynamic-update-slice_fusion.q_ref), channel_id=1, source_target_pairs={{0,28},{1,29},{2,30},{3,31},{4,0},{5,1},{6,2},{7,3},{8,4},{9,5},{1... | collective-permute-start | bytes 258056 | tf_op jit(solution)/shard_map/ppermute | solution.py:1056
  14.9 1.7 %collective-permute-done.5.qm_ref = f32[21,8,128]{2,1,0:T(8,128)S(1)} collective-permute-done((f32[21,8,128]{2,1,0:T(8,128)S(1)}, f32[21,8,128]{2,1,0:T(8,128)S(1)}, u32[]{:S(2)}, u32[]{:S(2)}) %collective-permute-start.5) | collective-permute-done | bytes 86048 | tf_op jit(solution)/shard_map/ppermute | solution.py:1056
  16.6 0.5 %collective-permute-done.4.sl_ref = f32[21,8,128]{2,1,0:T(8,128)S(1)} collective-permute-done((f32[21,8,128]{2,1,0:T(8,128)S(1)}, f32[21,8,128]{2,1,0:T(8,128)S(1)}, u32[]{:S(2)}, u32[]{:S(2)}) %collective-permute-start.4) | collective-permute-done | bytes 86048 | tf_op jit(solution)/shard_map/ppermute | solution.py:1056
  17.1 0.7 %collective-permute-done.3.qp_ref = f32[21,8,128]{2,1,0:T(8,128)S(1)} collective-permute-done((f32[21,8,128]{2,1,0:T(8,128)S(1)}, f32[21,8,128]{2,1,0:T(8,128)S(1)}, u32[]{:S(2)}, u32[]{:S(2)}) %collective-permute-start.3) | collective-permute-done | bytes 86048 | tf_op jit(solution)/shard_map/ppermute | solution.py:1056
  17.8 5.8 %shard_map.78 = (f32[2,8,128]{2,1,0:T(8,128)}, f32[8,128]{1,0:T(8,128)}) custom-call(f32[21,8,128]{2,1,0:T(8,128)S(1)} %collective-permute-done.3.qp_ref, f32[21,8,128]{2,1,0:T(8,128)S(1)} %collective-permute-done.4.sl_ref, f32[21,8,128]{2,1,0:T(8,128)S(1)} %collective-permute-done.5.qm_ref, f32[21,8,128]{2,1,0:T(8,128)S(1)} %constant_dynamic-update-slice_fusion.q_ref, ...), custom_call_target="tpu_custom_call" | custom-call | tf_op jit(solution)/shard_map/pallas_call | solution.py:1069
  (7 shorter events, 0.0 us)
Async XLA Ops:
  0.6 0.8 %copy-start.1 = (s32[2,1,8,128]{3,2,1,0:T(8,128)S(1)}, s32[2,1,8,128]{3,2,1,0:T(8,128)}, u32[]{:S(2)}) copy-start(s32[2,1,8,128]{3,2,1,0:T(8,128)} %param.6) | copy-start | bytes 24580
  0.6 0.8 %copy-start.2 = (s32[2,1,8,128]{3,2,1,0:T(8,128)S(1)}, s32[2,1,8,128]{3,2,1,0:T(8,128)}, u32[]{:S(2)}) copy-start(s32[2,1,8,128]{3,2,1,0:T(8,128)} %param.7) | copy-start | bytes 24580
  0.7 0.8 %copy-start.3 = (f32[2,1,8,128]{3,2,1,0:T(8,128)S(1)}, f32[2,1,8,128]{3,2,1,0:T(8,128)}, u32[]{:S(2)}) copy-start(f32[2,1,8,128]{3,2,1,0:T(8,128)} %param.8) | copy-start | bytes 24580
  0.7 0.8 %copy-start.4 = (f32[2,1,8,128]{3,2,1,0:T(8,128)S(1)}, f32[2,1,8,128]{3,2,1,0:T(8,128)}, u32[]{:S(2)}) copy-start(f32[2,1,8,128]{3,2,1,0:T(8,128)} %param.9) | copy-start | bytes 24580
  1.5 0.7 %copy-start.5 = (f32[2,1,8,128]{3,2,1,0:T(8,128)S(1)}, f32[2,1,8,128]{3,2,1,0:T(8,128)}, u32[]{:S(2)}) copy-start(f32[2,1,8,128]{3,2,1,0:T(8,128)} %param.10) | copy-start | bytes 24580
  2.2 3.0 %copy-start = (s32[1,8,128]{2,1,0:T(8,128)S(1)}, s32[1,8,128]{2,1,0:T(8,128)}, u32[]{:S(2)}) copy-start(s32[1,8,128]{2,1,0:T(8,128)} %param.11) | copy-start | bytes 12292
  2.2 4.8 %collective-permute-start = (f32[6,8,128]{2,1,0:T(8,128)S(1)}, f32[6,8,128]{2,1,0:T(8,128)S(1)}, u32[]{:S(2)}, u32[]{:S(2)}) collective-permute-start(f32[6,8,128]{2,1,0:T(8,128)S(1)} %pad_maximum_fusion.values_ref), channel_id=1, source_target_pairs={{0,1},{1,0},{2,3},{3,2},{4,5},{5,4},{6,7},{7,6},{8,9},{9,8},{10,11... | collective-permute-start | bytes 73736 | tf_op jit(solution)/shard_map/ppermute | solution.py:1056
  5.5 3.2 %collective-permute-start.2 = (f32[4,8,128]{2,1,0:T(8,128)S(1)}, f32[4,8,128]{2,1,0:T(8,128)S(1)}, u32[]{:S(2)}, u32[]{:S(2)}) collective-permute-start(f32[4,8,128]{2,1,0:T(8,128)S(1)} %get-tuple-element.6), channel_id=1, source_target_pairs={{0,3},{1,2},{2,1},{3,0},{4,7},{5,6},{6,5},{7,4},{8,11},{9,10},{10,... | collective-permute-start | bytes 49160 | tf_op jit(solution)/shard_map/ppermute | solution.py:1056
  5.5 1.5 %collective-permute-start.1 = (f32[4,8,128]{2,1,0:T(8,128)S(1)}, f32[4,8,128]{2,1,0:T(8,128)S(1)}, u32[]{:S(2)}, u32[]{:S(2)}) collective-permute-start(f32[4,8,128]{2,1,0:T(8,128)S(1)} %get-tuple-element.6), channel_id=1, source_target_pairs={{0,2},{1,3},{2,0},{3,1},{4,6},{5,7},{6,4},{7,5},{8,10},{9,11},{10,... | collective-permute-start | bytes 49160 | tf_op jit(solution)/shard_map/ppermute | solution.py:1056
  8.6 8.0 %collective-permute-start.5 = (f32[21,8,128]{2,1,0:T(8,128)S(1)}, f32[21,8,128]{2,1,0:T(8,128)S(1)}, u32[]{:S(2)}, u32[]{:S(2)}) collective-permute-start(f32[21,8,128]{2,1,0:T(8,128)S(1)} %constant_dynamic-update-slice_fusion.q_ref), channel_id=1, source_target_pairs={{0,4},{1,5},{2,6},{3,7},{4,8},{5,9},{6,10},{7,11},{8,12},{9,13},{1... | collective-permute-start | bytes 258056 | tf_op jit(solution)/shard_map/ppermute | solution.py:1056
  10.2 7.0 %collective-permute-start.4 = (f32[21,8,128]{2,1,0:T(8,128)S(1)}, f32[21,8,128]{2,1,0:T(8,128)S(1)}, u32[]{:S(2)}, u32[]{:S(2)}) collective-permute-start(f32[21,8,128]{2,1,0:T(8,128)S(1)} %constant_dynamic-update-slice_fusion.q_ref), channel_id=1, source_target_pairs={{0,8},{1,9},{2,26},{3,27},{4,12},{5,13},{6,30},{7,31},{8,16},{9,17... | collective-permute-start | bytes 258056 | tf_op jit(solution)/shard_map/ppermute | solution.py:1056
  11.7 6.0 %collective-permute-start.3 = (f32[21,8,128]{2,1,0:T(8,128)S(1)}, f32[21,8,128]{2,1,0:T(8,128)S(1)}, u32[]{:S(2)}, u32[]{:S(2)}) collective-permute-start(f32[21,8,128]{2,1,0:T(8,128)S(1)} %constant_dynamic-update-slice_fusion.q_ref), channel_id=1, source_target_pairs={{0,28},{1,29},{2,30},{3,31},{4,0},{5,1},{6,2},{7,3},{8,4},{9,5},{1... | collective-permute-start | bytes 258056 | tf_op jit(solution)/shard_map/ppermute | solution.py:1056
